TPU v7x, 512 devices: a whole 4x4x16 slice. The times are simulated.
512 devices in a mesh: dp: 4 (over y_hi, core), chan: 8 (over x, y_lo), seq: 16 (over z).
Axes of the slice: x: 4, y: 4 (y_hi: 2, y_lo: 2; y = y_hi * 2 + y_lo), z: 16, core: 2. Of those that a mesh axis runs over, the one named last changes fastest.
Arguments:
- query_input: bfloat16 [4, 2048, 8192], P('dp', 'seq', 'chan'), may hold values from -6 to 6
- key_input: bfloat16 [4, 2048, 8192], P('dp', 'seq', 'chan'), may hold values from -6 to 6
- value_input: bfloat16 [4, 2048, 8192], P('dp', 'seq', 'chan'), may hold values from -6 to 6
- grad_output: bfloat16 [4, 2048, 8192], P('dp', 'seq', 'chan'), may hold values from -6 to 6
- w_embed: float32 [32, 64], replicated, may hold values from -6 to 6
- w_filter: float32 [64, 8192], P(None, ('chan', 'seq')), may hold values from -0.1875 to 0.1875
- decay_rates: float32 [8192], P(('chan', 'seq')), may hold values from 0.1 to 122.88
Outputs:
- d_query: bfloat16 [4, 2048, 8192], P('dp', 'seq', 'chan')
- d_key: bfloat16 [4, 2048, 8192], P('dp', 'seq', 'chan')
- d_value: bfloat16 [4, 2048, 8192], P('dp', 'seq', 'chan')
- grad_filter: float32 [64, 8192], P(None, ('chan', 'seq'))
- grad_rate: float32 [8192], P(('chan', 'seq'))
- grad_embed: float32 [32, 64], replicated
All inputs are finite; a program needn't handle non-finite values.
Results may differ from a plain program's by a relative error of at most 0.0058.
Values may be sent and summed in bfloat16 or wider, within the bound.
No kernel may reach another device: no remote copies, remote signals or barrier semaphores. Data moves between devices by JAX's collectives and lax.ppermute only.
A program may use at most 64 MiB of HBM per device.

v0:
```python
import math

import jax
import jax.numpy as jnp
from jax import lax
from jax.sharding import PartitionSpec as P


def embed_features(positions, count, length):
    bands = jnp.arange(count // 2, dtype=jnp.float32) + 0.5
    phase = positions[None, :] * bands[:, None] * (2.0 * math.pi / length)
    return jnp.concatenate([jnp.sin(phase), jnp.cos(phase)], axis=0)


def angle_table(row_count, col_count, period):
    left = jnp.arange(row_count, dtype=jnp.float32)
    right = jnp.arange(col_count, dtype=jnp.float32)
    angles = jnp.outer(left, right) % period * (2.0 * math.pi / period)
    return (jnp.cos(angles), jnp.sin(angles))


def make_tables(half_outer, inner_size, fft_size):
    outer_size = 2 * half_outer
    outer_cos, outer_sin = angle_table(outer_size, outer_size, outer_size)
    twist_cos, twist_sin = angle_table(outer_size, inner_size, fft_size)
    inner_cos, inner_sin = angle_table(inner_size, inner_size, inner_size)
    first_table = jnp.stack([outer_cos[:half_outer], -outer_sin[:half_outer]], axis=1)
    last_forward = jnp.stack(
        [jnp.stack([inner_cos, -inner_sin], axis=1), jnp.stack([inner_sin, inner_cos], axis=1)],
        axis=0,
    )
    last_inverse = jnp.stack(
        [jnp.stack([inner_cos, inner_sin], axis=1), jnp.stack([-inner_sin, inner_cos], axis=1)],
        axis=0,
    )
    cos_head = outer_cos[:, :half_outer]
    sin_head = outer_sin[:, :half_outer]
    middle_both = jnp.stack(
        [jnp.stack([cos_head, sin_head], axis=1), jnp.stack([-sin_head, cos_head], axis=1)], axis=0
    )
    middle_real = jnp.stack([cos_head[:, None], -sin_head[:, None]], axis=0)
    return (first_table, twist_cos, twist_sin, last_forward, last_inverse, middle_both, middle_real)


def forward_spec(signal, tables, half_outer, inner_size):
    first_table, twist_cos, twist_sin, last_forward = (tables[0], tables[1], tables[2], tables[3])
    blocks = signal.reshape(signal.shape[0], half_outer, inner_size)
    first = jnp.einsum("cnm,nqk->cqkm", blocks, first_table, precision=lax.Precision.HIGHEST)
    part_real = first[:, 0]
    part_imag = first[:, 1]
    turned = jnp.stack(
        [
            part_real * twist_cos + part_imag * twist_sin,
            part_imag * twist_cos - part_real * twist_sin,
        ],
        axis=1,
    )
    return jnp.einsum("cpkm,pmqj->cqkj", turned, last_forward, precision=lax.Precision.HIGHEST)


def inverse_head(spec, tables, middle, fft_size):
    twist_cos, twist_sin, last_inverse = (tables[1], tables[2], tables[4])
    back = jnp.einsum("cpkm,pmqj->cqkj", spec, last_inverse, precision=lax.Precision.HIGHEST)
    back_real = back[:, 0]
    back_imag = back[:, 1]
    turned = jnp.stack(
        [
            back_real * twist_cos - back_imag * twist_sin,
            back_real * twist_sin + back_imag * twist_cos,
        ],
        axis=1,
    )
    times = jnp.einsum("cpkm,pkqn->cqnm", turned, middle, precision=lax.Precision.HIGHEST)
    return times.reshape(times.shape[0], times.shape[1], -1) / fft_size


def channel_work(conv_input, conv_upstream, filter_taps, half_outer, inner_size):
    length = conv_input.shape[1]
    fft_size = 2 * length
    tables = make_tables(half_outer, inner_size, fft_size)
    input_spec = forward_spec(conv_input, tables, half_outer, inner_size)
    upstream_spec = forward_spec(conv_upstream, tables, half_outer, inner_size)
    taps_spec = forward_spec(filter_taps, tables, half_outer, inner_size)
    input_real, input_imag = (input_spec[:, 0], input_spec[:, 1])
    upstream_real, upstream_imag = (upstream_spec[:, 0], upstream_spec[:, 1])
    taps_real, taps_imag = (taps_spec[:, 0], taps_spec[:, 1])
    conv_real = taps_real * input_real - taps_imag * input_imag
    conv_imag = taps_real * input_imag + taps_imag * input_real
    grad_real = taps_real * upstream_real + taps_imag * upstream_imag
    grad_imag = taps_real * upstream_imag - taps_imag * upstream_real
    joined = jnp.stack([conv_real - grad_imag, conv_imag + grad_real], axis=1)
    both = inverse_head(joined, tables, tables[5], fft_size)
    corr_real = input_real * upstream_real + input_imag * upstream_imag
    corr_imag = input_real * upstream_imag - input_imag * upstream_real
    correlation = inverse_head(
        jnp.stack([corr_real, corr_imag], axis=1), tables, tables[6], fft_size
    )
    return (both[:, 0], both[:, 1], correlation[:, 0])


def filter_grads(filter_grad, hidden_t, w_filter, window, filter_taps, positions, length):
    time_scale = 1.0 / math.sqrt(length)
    weighted = filter_grad * window
    grad_filter = (
        jnp.einsum("jt,ct->jc", hidden_t, weighted, precision=lax.Precision.HIGHEST) * time_scale
    )
    grad_rate = (
        -jnp.sum(positions[None, :] / length * filter_taps * filter_grad, axis=1) * time_scale
    )
    hidden_grad = jnp.einsum("jc,ct->jt", w_filter, weighted, precision=lax.Precision.HIGHEST)
    return (grad_filter, grad_rate, hidden_grad)


def embed_term(features_t, hidden_grad, pre_t, length):
    return jnp.einsum(
        "et,jt->ej", features_t, hidden_grad * jnp.cos(pre_t), precision=lax.Precision.HIGHEST
    ) * (1.0 / math.sqrt(length))


def per_device(query_input, key_input, value_input, grad_output, w_embed, w_filter, decay_rates):
    seq_count = lax.axis_size("seq")
    batch_count = lax.axis_size("dp")
    local_len = query_input.shape[1]
    length = local_len * seq_count
    query_all, key_all, value_all, grad_all = (
        lax.all_to_all(query_input, "seq", split_axis=2, concat_axis=1, tiled=True),
        lax.all_to_all(key_input, "seq", split_axis=2, concat_axis=1, tiled=True),
        lax.all_to_all(value_input, "seq", split_axis=2, concat_axis=1, tiled=True),
        lax.all_to_all(grad_output, "seq", split_axis=2, concat_axis=1, tiled=True),
    )
    product = (key_all.astype(jnp.float32) * value_all.astype(jnp.float32)).astype(jnp.bfloat16)
    upstream = (grad_all.astype(jnp.float32) * query_all.astype(jnp.float32)).astype(jnp.bfloat16)
    product, upstream = lax.optimization_barrier((product, upstream))
    conv_input = product[0].T.astype(jnp.float32)
    conv_upstream = upstream[0].T.astype(jnp.float32)
    positions = jnp.arange(length, dtype=jnp.float32)
    features_t = embed_features(positions, w_embed.shape[0], length)
    pre_t = jnp.einsum("ej,et->jt", w_embed, features_t, precision=lax.Precision.HIGHEST)
    hidden_t = jnp.sin(pre_t)
    window = jnp.exp(-decay_rates[:, None] * positions[None, :] / length)
    filter_taps = (
        jnp.einsum("jc,jt->ct", w_filter, hidden_t, precision=lax.Precision.HIGHEST) * window
    )
    conv_out, conv_grad, correlation = channel_work(
        conv_input, conv_upstream, filter_taps, seq_count, local_len
    )
    correlation = correlation * (1.0 / math.sqrt(batch_count * length))
    conv_send = conv_out.T[None].astype(jnp.bfloat16)
    grad_send = conv_grad.T[None].astype(jnp.bfloat16)
    conv_send, grad_send = lax.optimization_barrier((conv_send, grad_send))
    conv_wide = conv_send.astype(jnp.float32)
    grad_wide = grad_send.astype(jnp.float32)
    d_query = (grad_all.astype(jnp.float32) * conv_wide).astype(jnp.bfloat16)
    d_key = (grad_wide * value_all.astype(jnp.float32)).astype(jnp.bfloat16)
    d_value = (grad_wide * key_all.astype(jnp.float32)).astype(jnp.bfloat16)
    d_query, d_key, d_value = (
        lax.all_to_all(d_query, "seq", split_axis=1, concat_axis=2, tiled=True),
        lax.all_to_all(d_key, "seq", split_axis=1, concat_axis=2, tiled=True),
        lax.all_to_all(d_value, "seq", split_axis=1, concat_axis=2, tiled=True),
    )
    summed = lax.psum(correlation, "dp")
    grad_filter, grad_rate, hidden_grad = filter_grads(
        summed, hidden_t, w_filter, window, filter_taps, positions, length
    )
    hidden_grad = lax.psum(hidden_grad, ("chan", "seq"))
    grad_embed = embed_term(features_t, hidden_grad, pre_t, length)
    return (d_query, d_key, d_value, grad_filter, grad_rate, grad_embed)


def solution(mesh):
    in_specs = (
        P("dp", "seq", "chan"),
        P("dp", "seq", "chan"),
        P("dp", "seq", "chan"),
        P("dp", "seq", "chan"),
        P(),
        P(None, ("chan", "seq")),
        P(("chan", "seq")),
    )
    out_specs = (
        P("dp", "seq", "chan"),
        P("dp", "seq", "chan"),
        P("dp", "seq", "chan"),
        P(None, ("chan", "seq")),
        P(("chan", "seq")),
        P(),
    )
    return jax.shard_map(
        per_device, mesh=mesh, in_specs=in_specs, out_specs=out_specs, check_vma=False
    )
```

profile of v0, /device:TPU:32, one launch (start us, length us, event | category | flops | bytes accessed | tf_op | source)
XLA Modules:
  0.0 1377.3 jit_solution(2234027452655575021)
XLA Ops:
  7.2 1.3 copy.224
  9.0 2.2 reduce
  11.2 0.8 reshape.271
  12.0 15.2 %all-to-all-start = ((bf16[16,2,4096]{2,1,0:T(2,128)(2,1)}), bf16[16,2,4096]{2,1,0:T(2,128)(2,1)S(1)}, u32[]{:S(2)}, u32[]{:S(2)}) async-start(bf16[16,2,4096]{2,1,0:T(2,128)(2,1)} %reshape.271), calls=%async_computation | async-start | bytes 524288 | tf_op jit(solution)/shard_map/all_to_all | solution.py:129
  27.6 2.2 reduce.2
  31.0 2.2 reduce.3
  33.3 0.8 reshape.275
  34.5 2.2 reduce.1
  37.5 7.7 all-to-all-done
  45.1 6.3 all-to-all-start.1
  52.0 3.2 fusion.112
  55.8 0.8 copy-done.1
  56.9 12.0 all-to-all-done.1
  68.9 6.6 all-to-all-start.2
  77.5 15.5 %all-to-all-done.2 = bf16[16,2,4096]{2,1,0:T(2,128)(2,1)S(1)} async-done(((bf16[16,2,4096]{2,1,0:T(2,128)(2,1)}), bf16[16,2,4096]{2,1,0:T(2,128)(2,1)S(1)}, u32[]{:S(2)}, u32[]{:S(2)}) %all-to-all-start.2) | async-done | bytes 262176 | tf_op jit(solution)/shard_map/all_to_all | solution.py:128
  93.0 6.6 all-to-all-start.3
  99.6 1.8 convolution_bitcast_fusion.4
  101.8 1.1 copy.226
  102.9 2.2 reshape.274
  105.5 2.2 reshape.276
  108.1 9.1 all-to-all-done.3
  117.2 2.8 reshape.278
  120.0 1.1 copy.236
  121.5 1.6 multiply_convert_fusion
  123.4 1.0 convolution_bitcast_fusion.2
  124.6 1.0 convolution_bitcast_fusion.3
  125.6 0.9 multiply_add_fusion.4
  126.9 3.3 fusion.21
  130.2 3.3 fusion.24
  133.8 12.1 fusion.27
  146.5 1.0 subtract_subtract_fusion
  148.7 3.2 fusion.30
  151.9 3.2 fusion.33
  155.1 1.2 multiply_subtract_fusion
  156.4 2.0 fusion.48
  158.3 2.1 reshape.241
  160.4 1.8 slice_bitcast_fusion
  162.2 1.1 fusion.55
  163.3 2.3 copy.254
  165.5 12.3 reduce.6
  177.9 2.1 reshape.283
  180.0 6.6 all-to-all-start.6
  187.4 12.3 reduce.5
  199.7 2.1 reshape.281
  201.8 2.4 all-to-all-done.6
  204.2 9.7 all-to-all-start.5
  214.0 1.1 fusion.51
  215.1 1.0 copy.354
  216.3 0.9 copy.246
  217.2 11.6 reduce.4
  228.8 1.1 reshape.279
  229.9 1.6 all-to-all-done.5
  231.5 10.4 all-to-all-start.4
  242.0 34.1 %all-reduce.3.cloned.1.call-done = f32[64,2048]{1,0:T(8,128)} async-done(((f32[64,2048]{1,0:T(8,128)}), f32[64,2048]{1,0:T(8,128)}) %all-reduce.3.cloned.1.call-update) | async-done | bytes 524304 | tf_op jit(solution)/shard_map/psum | solution.py:161
  276.1 2.7 convolution_bitcast_fusion
  278.8 1.2 multiply_reduce_fusion
  280.6 1.4 convolution_multiply_fusion
  281.9 2.1 reshape.284
  284.8 0.9 copy.264
  285.7 2.1 reshape.282
  288.6 0.9 copy.263
  290.8 0.9 copy.262
  291.7 1074.7 %all-reduce.5.cloned.1.call-done = f32[64,2048]{1,0:T(8,128)} async-done(((f32[64,2048]{1,0:T(8,128)}), f32[64,2048]{1,0:T(8,128)}) %all-reduce.5.cloned.1.call-update) | async-done | bytes 524304 | tf_op jit(solution)/shard_map/psum | solution.py:165
  1366.4 3.8 convolution_multiply_fusion.1
  (115 shorter events, 15.4 us)
Async XLA Ops:
  7.2 48.0 %copy-start = (f32[64,64]{1,0:T(8,128)S(1)}, f32[64,64]{1,0:T(8,128)}, u32[]{:S(2)}) copy-start(f32[64,64]{1,0:T(8,128)} %param.12) | copy-start | bytes 49156
  7.2 20.0 %copy-start.19 = (bf16[1,128,1024]{2,1,0:T(8,128)(2,1)S(1)}, bf16[1,128,1024]{2,1,0:T(8,128)(2,1)}, u32[]{:S(2)}) copy-start(bf16[1,128,1024]{2,1,0:T(8,128)(2,1)} %param.8) | copy-start | bytes 786436
  8.5 22.1 %copy-start.20 = (bf16[1,128,1024]{2,1,0:T(8,128)(2,1)S(1)}, bf16[1,128,1024]{2,1,0:T(8,128)(2,1)}, u32[]{:S(2)}) copy-start(bf16[1,128,1024]{2,1,0:T(8,128)(2,1)} %param.9) | copy-start | bytes 786436
  12.0 33.1 %all-to-all-start = ((bf16[16,2,4096]{2,1,0:T(2,128)(2,1)}), bf16[16,2,4096]{2,1,0:T(2,128)(2,1)S(1)}, u32[]{:S(2)}, u32[]{:S(2)}) async-start(bf16[16,2,4096]{2,1,0:T(2,128)(2,1)} %reshape.271), calls=%async_computation | async-start | bytes 524288 | tf_op jit(solution)/shard_map/all_to_all | solution.py:129
  27.2 6.8 copy-start.21
  30.6 6.8 copy-start.27
  31.0 20.9 %copy-start.24 = (f32[32,64]{1,0:T(8,128)S(1)}, f32[32,64]{1,0:T(8,128)}, u32[]{:S(2)}) copy-start(f32[32,64]{1,0:T(8,128)} %param.11) | copy-start | bytes 24580
  37.5 18.3 %copy-start.25 = (f32[64]{0:T(128)}, f32[64]{0:T(128)S(1)}, u32[]{:S(2)}) copy-start(f32[64]{0:T(128)S(1)} %neg.33) | copy-start | bytes 772
  45.1 23.8 %all-to-all-start.1 = ((bf16[16,2,4096]{2,1,0:T(2,128)(2,1)}), bf16[16,2,4096]{2,1,0:T(2,128)(2,1)S(1)}, u32[]{:S(2)}, u32[]{:S(2)}) async-start(bf16[16,2,4096]{2,1,0:T(2,128)(2,1)} %reshape.273), calls=%async_computation.1 | async-start | bytes 524288 | tf_op jit(solution)/shard_map/all_to_all | solution.py:127
  51.9 3.2 copy-start.11
  52.0 3.2 copy-start.13
  55.1 1.6 copy-start.6
  55.8 0.8 copy-start.1
  68.9 7.9 copy-start.16
  68.9 24.1 %all-to-all-start.2 = ((bf16[16,2,4096]{2,1,0:T(2,128)(2,1)}), bf16[16,2,4096]{2,1,0:T(2,128)(2,1)S(1)}, u32[]{:S(2)}, u32[]{:S(2)}) async-start(bf16[16,2,4096]{2,1,0:T(2,128)(2,1)} %reshape.275), calls=%async_computation.2 | async-start | bytes 524288 | tf_op jit(solution)/shard_map/all_to_all | solution.py:128
  93.0 8.7 copy-start.17
  93.0 24.2 %all-to-all-start.3 = ((bf16[16,2,4096]{2,1,0:T(2,128)(2,1)}), bf16[16,2,4096]{2,1,0:T(2,128)(2,1)}, u32[]{:S(2)}, u32[]{:S(2)}) async-start(bf16[16,2,4096]{2,1,0:T(2,128)(2,1)} %reshape.277), calls=%async_computation.3 | async-start | bytes 524288 | tf_op jit(solution)/shard_map/all_to_all | solution.py:126
  120.0 1.5 copy-start.3
  147.7 0.9 copy-start.9
  147.7 1.0 copy-start.10
  163.3 23.3 %copy-start.15 = (bf16[1,2048,64]{1,2,0:T(8,128)(2,1)S(1)}, bf16[1,2048,64]{1,2,0:T(8,128)(2,1)}, u32[]{:S(2)}) copy-start(bf16[1,2048,64]{1,2,0:T(8,128)(2,1)} %get-tuple-element.73) | copy-start | bytes 786436
  180.0 24.2 %all-to-all-start.6 = ((bf16[16,2,4096]{2,1,0:T(2,128)(2,1)}), bf16[16,2,4096]{2,1,0:T(2,128)(2,1)}, u32[]{:S(2)}, u32[]{:S(2)}) async-start(bf16[16,2,4096]{2,1,0:T(2,128)(2,1)} %reshape.283), calls=%async_computation.6 | async-start | bytes 524288 | tf_op jit(solution)/shard_map/all_to_all | solution.py:159
  186.6 27.3 %copy-start.22 = (f32[1,32,1,16]{3,1,2,0:T(8,128)S(1)}, f32[1,32,1,16]{3,1,2,0:T(8,128)}, u32[]{:S(2)}) copy-start(f32[1,32,1,16]{3,1,2,0:T(8,128)} %get-tuple-element.86) | copy-start | bytes 6148
  186.6 27.3 %copy-start.23 = (f32[1,32,1,16]{3,1,2,0:T(8,128)S(1)}, f32[1,32,1,16]{3,1,2,0:T(8,128)}, u32[]{:S(2)}) copy-start(f32[1,32,1,16]{3,1,2,0:T(8,128)} %get-tuple-element.107) | copy-start | bytes 6148
  204.2 27.3 %all-to-all-start.5 = ((bf16[16,2,4096]{2,1,0:T(2,128)(2,1)}), bf16[16,2,4096]{2,1,0:T(2,128)(2,1)}, u32[]{:S(2)}, u32[]{:S(2)}) async-start(bf16[16,2,4096]{2,1,0:T(2,128)(2,1)} %reshape.281), calls=%async_computation.5 | async-start | bytes 524288 | tf_op jit(solution)/shard_map/all_to_all | solution.py:158
  213.9 62.3 %all-reduce.3.cloned.1.call-start = ((), (), s32[]{:S(2)}) async-start(), calls=%async_computation.7 | async-start | bytes 1048576 | tf_op jit(solution)/shard_map/psum | solution.py:161
  213.9 2.1 copy-start.4
  213.9 2.1 copy-start.18
  216.3 59.9 %copy-start.26 = (f32[64]{0:T(128)S(1)}, f32[64]{0:T(128)}, u32[]{:S(2)}) copy-start(f32[64]{0:T(128)} %copy-done.25) | copy-start | bytes 772
  217.2 61.7 %copy-start.2 = (f32[64,2048]{1,0:T(8,128)S(1)}, f32[64,2048]{1,0:T(8,128)}, u32[]{:S(2)}) copy-start(f32[64,2048]{1,0:T(8,128)} %copy-done.1) | copy-start | bytes 1572868
  228.8 51.8 %copy-start.7 = (f32[2048,64]{0,1:T(8,128)S(1)}, f32[2048,64]{0,1:T(8,128)}, u32[]{:S(2)}) copy-start(f32[2048,64]{0,1:T(8,128)} %copy-done.6) | copy-start | bytes 1572868
  231.5 57.9 %all-to-all-start.4 = ((bf16[16,2,4096]{2,1,0:T(2,128)(2,1)}), bf16[16,2,4096]{2,1,0:T(2,128)(2,1)S(1)}, u32[]{:S(2)}, u32[]{:S(2)}) async-start(bf16[16,2,4096]{2,1,0:T(2,128)(2,1)} %reshape.279), calls=%async_computation.4 | async-start | bytes 524288 | tf_op jit(solution)/shard_map/all_to_all | solution.py:157
  241.9 1124.5 %all-reduce.5.cloned.1.call-start = ((), (), s32[]{:S(2)}) async-start(), calls=%async_computation.8 | async-start | bytes 1048576 | tf_op jit(solution)/shard_map/psum | solution.py:165
  276.1 4.4 copy-start.5
  289.4 1077.0 %copy-start.8 = (f32[2048,64]{0,1:T(8,128)S(1)}, f32[2048,64]{0,1:T(8,128)}, u32[]{:S(2)}) copy-start(f32[2048,64]{0,1:T(8,128)} %get-tuple-element.96) | copy-start | bytes 1572868
  289.4 1077.0 %copy-start.12 = (f32[16,2048]{1,0:T(8,128)S(1)}, f32[16,2048]{1,0:T(8,128)}, u32[]{:S(2)}) copy-start(f32[16,2048]{1,0:T(8,128)} %copy-done.11) | copy-start | bytes 393220
  289.4 1077.0 %copy-start.14 = (f32[16,2048]{1,0:T(8,128)S(1)}, f32[16,2048]{1,0:T(8,128)}, u32[]{:S(2)}) copy-start(f32[16,2048]{1,0:T(8,128)} %copy-done.13) | copy-start | bytes 393220
Sparse Core Ops, SparseCore 0:
  217.6 58.4 all-reduce.2
  279.0 1087.3 all-reduce.4
where the time goes:
time: 1390 us; the launch traced here: 1380 us
  waiting for transfers between devices  1160 us (83%)
  starting transfers between devices  61.3 us (4%)
  other arithmetic  57.5 us (4%)
  matrix products  43.8 us (3%)
  local copies, waits for them, and re-layouts  42.5 us (3%)
  between operations  15 us (1%)
    psum x1, waiting for transfers between devices, per_device(): hidden_grad = lax.psum(hidden_grad, ('chan', 'seq'))  1070 us
    unnamed x7, other arithmetic  45.1 us
    psum x1, waiting for transfers between devices, per_device(): summed = lax.psum(correlation, 'dp')  34.1 us
    unnamed x87, local copies, waits for them, and re-layouts  29.5 us
  transfers between devices with their start and end apart: 9, of which 8 were waited for; matrix products, arithmetic and copies ran while one was open for 5% of the time, Pallas kernels for 0%

commit v1 on v0

v1 whole, which is shorter than its diff:
```python
import math

import jax
import jax.numpy as jnp
import numpy as np
from jax import lax
from jax.experimental import pallas as pl
from jax.experimental.pallas import tpu as pltpu
from jax.sharding import PartitionSpec as P

BLOCKS = 16
INNER = 128
GROUP = 64
HALF = 17
LENGTH = BLOCKS * INNER
PERIOD = 2 * LENGTH
VMEM = pl.BlockSpec(memory_space=pltpu.VMEM)
PARAMS = pltpu.CompilerParams(vmem_limit_bytes=40 * 1024 * 1024)


def split_table(table):
    high = table.astype(jnp.bfloat16)
    low = (table - high.astype(np.float64)).astype(jnp.bfloat16)
    return np.stack([high, low])


def tables():
    inner = np.arange(INNER)
    angle = 2.0 * math.pi * (np.outer(inner, inner) % INNER) / INNER
    cos, sin = np.cos(angle), np.sin(angle)
    forward = np.block([[cos, -sin], [sin, cos]])
    inverse = np.block([[cos, sin], [-sin, cos]])
    turn = 2.0 * math.pi * np.outer(np.arange(HALF), inner) / PERIOD
    weight = np.full((HALF, 1), 2.0 / PERIOD)
    weight[0] = weight[-1] = 1.0 / PERIOD
    twist = np.stack([np.cos(turn), np.sin(turn)], axis=1).astype(np.float32)
    untwist = np.stack([np.cos(turn) * weight, np.sin(turn) * weight], axis=1).astype(np.float32)
    return split_table(forward), split_table(inverse), twist, untwist


def embed_features(count):
    bands = np.arange(count // 2) + 0.5
    phase = np.arange(LENGTH)[None, :] * bands[:, None] * (2.0 * math.pi / LENGTH)
    return np.concatenate([np.sin(phase), np.cos(phase)], axis=0).astype(np.float32)


def weighted_sum(terms):
    total = None
    for value, factor in terms:
        if abs(factor) < 1e-9:
            continue
        if abs(factor - 1.0) < 1e-9:
            total = value if total is None else total + value
        elif abs(factor + 1.0) < 1e-9:
            total = -value if total is None else total - value
        else:
            part = value * np.float32(factor)
            total = part if total is None else total + part
    return total


def odd_bins(x):
    size = len(x)
    half = size // 2
    if size == 2:
        return {1: (x[0], -x[1])}
    minus = {n: x[n] - x[size - n] for n in range(1, half)}
    plus = {n: x[n] + x[size - n] for n in range(1, half)}
    minus[0] = x[0]
    plus[half] = x[half]
    out = {}
    for k in range(1, half, 2):
        cos = lambda n: math.cos(math.pi * k * n / size)
        sin = lambda n: math.sin(math.pi * k * n / size)
        cos_even = weighted_sum([(minus[n], cos(n)) for n in range(0, half, 2)])
        cos_odd = weighted_sum([(minus[n], cos(n)) for n in range(1, half, 2)])
        sin_even = weighted_sum([(plus[n], sin(n)) for n in range(2, half + 1, 2)])
        sin_odd = weighted_sum([(plus[n], sin(n)) for n in range(1, half, 2)])
        out[k] = (cos_even + cos_odd, -(sin_even + sin_odd))
        out[size - k] = (cos_even - cos_odd, sin_even - sin_odd)
    return out


def real_bins(x):
    size = len(x)
    half = size // 2
    if size == 2:
        return {0: (x[0] + x[1], None), 1: (x[0] - x[1], None)}
    out = {2 * k: v for k, v in real_bins([x[n] + x[n + half] for n in range(half)]).items()}
    out.update(odd_bins([x[n] - x[n + half] for n in range(half)]))
    return out


def outer_bins(x):
    out = {2 * k: v for k, v in real_bins(x).items()}
    out.update(odd_bins(x))
    return out


def odd_times(bins, size):
    half = size // 2
    if size == 2:
        return [bins[1][0], -bins[1][1]]
    ks = range(1, half, 2)
    real_plus = {k: bins[k][0] + bins[size - k][0] for k in ks}
    real_minus = {k: bins[k][0] - bins[size - k][0] for k in ks}
    imag_plus = {k: bins[k][1] + bins[size - k][1] for k in ks}
    imag_minus = {k: bins[k][1] - bins[size - k][1] for k in ks}
    out = [None] * size
    for n in range(half + 1):
        reals, imags = (real_minus, imag_plus) if n % 2 else (real_plus, imag_minus)
        cos = weighted_sum([(reals[k], math.cos(math.pi * k * n / size)) for k in ks])
        sin = weighted_sum([(imags[k], math.sin(math.pi * k * n / size)) for k in ks])
        if n == 0:
            out[0] = cos
        elif n == half:
            out[half] = -sin
        else:
            out[n] = cos - sin
            out[size - n] = -(cos + sin)
    return out


def real_times(bins, size):
    if size == 2:
        return [bins[0][0] + bins[1][0], bins[0][0] - bins[1][0]]
    half = size // 2
    even = real_times({k // 2: v for k, v in bins.items() if k % 2 == 0}, half)
    odd = odd_times({k: v for k, v in bins.items() if k % 2}, half)
    return [even[n] + odd[n] for n in range(half)] + [even[n] - odd[n] for n in range(half)]


def outer_times(bins, size):
    even = real_times({k // 2: v for k, v in bins.items() if k % 2 == 0}, size)
    odd = odd_times({k: v for k, v in bins.items() if k % 2}, size)
    return [even[n] + odd[n] for n in range(size)]


def precise_dot(values, table_ref):
    high = values.astype(jnp.bfloat16)
    low = (values - high.astype(jnp.float32)).astype(jnp.bfloat16)
    dot = lambda a, b: jnp.dot(a, b, preferred_element_type=jnp.float32)
    return dot(high, table_ref[0]) + (dot(low, table_ref[0]) + dot(high, table_ref[1]))


def forward_outer(load, rows, twist_ref, turned_ref):
    @pl.loop(0, rows // 8)
    def _(step):
        where = pl.ds(pl.multiple_of(step * 8, 8), 8)
        bins = outer_bins([load(n, where) for n in range(BLOCKS)])
        for k in range(HALF):
            real, imag = bins[k]
            cos, sin = twist_ref[k, 0:1, :], twist_ref[k, 1:2, :]
            if k == 0:
                turned_real, turned_imag = real, jnp.zeros_like(real)
            elif imag is None:
                turned_real, turned_imag = real * cos, -real * sin
            else:
                turned_real, turned_imag = real * cos + imag * sin, imag * cos - real * sin
            turned_ref[k, where, :INNER] = turned_real
            turned_ref[k, where, INNER:] = turned_imag


def inverse_outer(back_ref, rows, untwist_ref, store):
    @pl.loop(0, rows // 8)
    def _(step):
        where = pl.ds(pl.multiple_of(step * 8, 8), 8)
        bins = {}
        for k in range(HALF):
            real, imag = back_ref[k, where, :INNER], back_ref[k, where, INNER:]
            cos, sin = untwist_ref[k, 0:1, :], untwist_ref[k, 1:2, :]
            if k in (0, HALF - 1):
                bins[k] = (real * cos - imag * sin, None)
            else:
                bins[k] = (real * cos - imag * sin, real * sin + imag * cos)
        for n, value in enumerate(outer_times(bins, BLOCKS)):
            store(n, where, value)


def pack_kernel(query_ref, key_ref, value_ref, grad_ref, sent_ref):
    for first, second, place in ((key_ref, value_ref, 0), (grad_ref, query_ref, GROUP)):
        for pair in range(BLOCKS // 2):
            lanes = slice(2 * GROUP * pair, 2 * GROUP * (pair + 1))
            both = first[0, :, lanes].astype(jnp.float32) * second[0, :, lanes].astype(jnp.float32)
            both = both.T.astype(jnp.bfloat16)
            sent_ref[2 * pair, place : place + GROUP] = both[:GROUP]
            sent_ref[2 * pair + 1, place : place + GROUP] = both[GROUP:]


def filter_kernel(
    hidden_ref, filter_ref, rate_ref, table_ref, twist_ref, window_ref, taps_ref, spec_ref, turned_ref
):
    positions = lax.broadcasted_iota(jnp.int32, (1, LENGTH), 1).astype(jnp.float32)
    window = jnp.exp(-rate_ref[...] * positions / LENGTH)
    window_ref[...] = window
    taps_ref[...] = window * lax.dot_general(
        filter_ref[...],
        hidden_ref[...],
        (((0,), (0,)), ((), ())),
        precision=lax.Precision.HIGHEST,
        preferred_element_type=jnp.float32,
    )
    forward_outer(
        lambda n, where: taps_ref[where, n * INNER : (n + 1) * INNER], GROUP, twist_ref, turned_ref
    )
    turned = turned_ref[...].reshape(HALF * GROUP, 2 * INNER)
    spec_ref[...] = precise_dot(turned, table_ref).reshape(HALF, GROUP, 2 * INNER)


def conv_kernel(
    got_ref, taps_ref, table_ref, back_table_ref, twist_ref, untwist_ref, out_ref, corr_ref, wide_ref, turned_ref, back_ref
):
    wide_ref[...] = got_ref[...].astype(jnp.float32)
    forward_outer(lambda n, where: wide_ref[n, where, :], 2 * GROUP, twist_ref, turned_ref)
    for first, last in ((0, 4), (4, 8), (8, 12), (12, HALF)):
        count = last - first
        turned = turned_ref[first:last].reshape(count * 2 * GROUP, 2 * INNER)
        spec = precise_dot(turned, table_ref).reshape(count, 2 * GROUP, 2 * INNER)
        in_real, in_imag = spec[:, :GROUP, :INNER], spec[:, :GROUP, INNER:]
        up_real, up_imag = spec[:, GROUP:, :INNER], spec[:, GROUP:, INNER:]
        tap_real, tap_imag = taps_ref[first:last, :, :INNER], taps_ref[first:last, :, INNER:]
        joined = jnp.concatenate(
            [
                jnp.concatenate(
                    [tap_real * in_real - tap_imag * in_imag, tap_real * in_imag + tap_imag * in_real],
                    axis=2,
                ),
                jnp.concatenate(
                    [tap_real * up_real + tap_imag * up_imag, tap_real * up_imag - tap_imag * up_real],
                    axis=2,
                ),
            ],
            axis=1,
        )
        corr_ref[first:last, :, :INNER] = in_real * up_real + in_imag * up_imag
        corr_ref[first:last, :, INNER:] = in_real * up_imag - in_imag * up_real
        back = precise_dot(joined.reshape(count * 2 * GROUP, 2 * INNER), back_table_ref)
        back_ref[first:last] = back.reshape(count, 2 * GROUP, 2 * INNER)

    def store(n, where, value):
        wide_ref[n, where, :] = value

    inverse_outer(back_ref, 2 * GROUP, untwist_ref, store)
    out_ref[...] = wide_ref[...].astype(jnp.bfloat16)


def grads_kernel(
    corr_ref, hidden_ref, slope_ref, features_ref, filter_ref, window_ref, taps_ref, back_table_ref, untwist_ref,
    grads_ref, back_ref, corr_time_ref,
):
    back = precise_dot(corr_ref[...].reshape(HALF * GROUP, 2 * INNER), back_table_ref)
    back_ref[...] = back.reshape(HALF, GROUP, 2 * INNER)
    batch_scale = np.float32(1.0 / math.sqrt(4 * LENGTH))
    time_scale = np.float32(1.0 / math.sqrt(LENGTH))

    def store(n, where, value):
        corr_time_ref[where, n * INNER : (n + 1) * INNER] = value * batch_scale

    inverse_outer(back_ref, GROUP, untwist_ref, store)
    corr = corr_time_ref[...]
    weighted = corr * window_ref[...]
    nt = (((1,), (1,)), ((), ()))
    exact = dict(precision=lax.Precision.HIGHEST, preferred_element_type=jnp.float32)
    grads_ref[:, :GROUP] = lax.dot_general(hidden_ref[...], weighted, nt, **exact) * time_scale
    hidden_grad = jnp.dot(filter_ref[...], weighted, **exact) * slope_ref[...]
    grads_ref[:32, GROUP:] = lax.dot_general(features_ref[...], hidden_grad, nt, **exact) * time_scale
    positions = lax.broadcasted_iota(jnp.int32, (1, LENGTH), 1).astype(jnp.float32)
    rate = positions / LENGTH * taps_ref[...] * corr
    ones = jnp.full((32, LENGTH), -time_scale, jnp.float32)
    grads_ref[32:, GROUP:] = lax.dot_general(ones, rate, nt, **exact)


def apply_kernel(got_ref, key_ref, value_ref, grad_ref, d_query_ref, d_key_ref, d_value_ref):
    for pair in range(BLOCKS // 2):
        lanes = slice(2 * GROUP * pair, 2 * GROUP * (pair + 1))

        def times(place):
            both = [got_ref[2 * pair + i, place : place + GROUP].astype(jnp.float32) for i in (0, 1)]
            return jnp.concatenate(both, axis=0).T

        conv, grad = times(0), times(GROUP)
        d_query_ref[0, :, lanes] = (grad_ref[0, :, lanes].astype(jnp.float32) * conv).astype(jnp.bfloat16)
        d_key_ref[0, :, lanes] = (grad * value_ref[0, :, lanes].astype(jnp.float32)).astype(jnp.bfloat16)
        d_value_ref[0, :, lanes] = (grad * key_ref[0, :, lanes].astype(jnp.float32)).astype(jnp.bfloat16)


def call(kernel, outs, ins, scratch=()):
    return pl.pallas_call(
        kernel,
        out_shape=[jax.ShapeDtypeStruct(shape, dtype) for shape, dtype in outs],
        in_specs=[VMEM] * len(ins),
        out_specs=[VMEM] * len(outs),
        scratch_shapes=[pltpu.VMEM(shape, jnp.float32) for shape in scratch],
        compiler_params=PARAMS,
    )(*ins)


def swapped_sum(value, axis, step):
    size = lax.axis_size(axis)
    return value + lax.ppermute(value, axis, [(i, i ^ step) for i in range(size)])


def per_device(query_input, key_input, value_input, grad_output, w_embed, w_filter, decay_rates):
    f32, bf16 = jnp.float32, jnp.bfloat16
    forward, inverse, twist, untwist = (jnp.asarray(t) for t in tables())
    features = jnp.asarray(embed_features(w_embed.shape[0]))
    spectrum = (HALF, GROUP, 2 * INNER)
    both = (HALF, 2 * GROUP, 2 * INNER)
    moved = (BLOCKS, 2 * GROUP, INNER)
    flat = (GROUP, LENGTH)
    (sent,) = call(
        pack_kernel, [(moved, bf16)], (query_input, key_input, value_input, grad_output)
    )
    got = lax.all_to_all(sent, "seq", split_axis=0, concat_axis=0, tiled=True)
    pre = jnp.einsum("ej,et->jt", w_embed, features, precision=lax.Precision.HIGHEST)
    hidden, slope = jnp.sin(pre), jnp.cos(pre)
    window, taps, taps_spec = call(
        filter_kernel,
        [(flat, f32), (flat, f32), (spectrum, f32)],
        (hidden, w_filter, decay_rates[:, None], forward, twist),
        [spectrum],
    )
    result, corr = call(
        conv_kernel,
        [(moved, bf16), (spectrum, f32)],
        (got, taps_spec, forward, inverse, twist, untwist),
        [moved, both, both],
    )
    back = lax.all_to_all(result, "seq", split_axis=0, concat_axis=0, tiled=True)
    (grads,) = call(
        grads_kernel,
        [((GROUP, 2 * GROUP), f32)],
        (corr, hidden, slope, features, w_filter, window, taps, inverse, untwist),
        [spectrum, flat],
    )
    grads = swapped_sum(swapped_sum(grads, "dp", 1), "dp", 2)
    embed = grads[:32, GROUP:]
    for step in (1, 2, 4):
        embed = swapped_sum(embed, "chan", step)
    d_query, d_key, d_value = call(
        apply_kernel,
        [(query_input.shape, bf16)] * 3,
        (back, key_input, value_input, grad_output),
    )
    embed, _ = lax.optimization_barrier((embed, back))
    everyone = jnp.broadcast_to(embed[None], (BLOCKS,) + embed.shape)
    grad_embed = jnp.sum(
        lax.all_to_all(everyone, "seq", split_axis=0, concat_axis=0, tiled=True), axis=0
    )
    return (d_query, d_key, d_value, grads[:, :GROUP], grads[32, GROUP:], grad_embed)


def solution(mesh):
    wide = P("dp", "seq", "chan")
    split = ("chan", "seq")
    return jax.shard_map(
        per_device,
        mesh=mesh,
        in_specs=(wide, wide, wide, wide, P(), P(None, split), P(split)),
        out_specs=(wide, wide, wide, P(None, split), P(split), P()),
        check_vma=False,
    )
```

time: 1390 us -> 127 us (0.09)
  the two profiles are of different devices: /device:TPU:32 before, /device:TPU:10 now
where the time goes in v1:
time: 127 us; the launch traced here: 126 us
  starting transfers between devices  48.8 us (38%)
  waiting for transfers between devices  46.3 us (36%)
  local copies, waits for them, and re-layouts  12.9 us (10%)
  Pallas kernels  11.6 us (9%)
  matrix products  3.92 us (3%)
  other arithmetic  1.68 us (1%)
    all_to_all x1, waiting for transfers between devices, per_device(): got = lax.all_to_all(sent, 'seq', split_axis=0, concat_axis=0, tiled=True)  21.1 us
    all_to_all x1, starting transfers between devices, per_device(): got = lax.all_to_all(sent, 'seq', split_axis=0, concat_axis=0, tiled=True)  15.3 us
    ppermute x5, starting transfers between devices, swapped_sum(): lax.ppermute(value, axis, [(i, i ^ step) for i in range(size)])  15 us
    ppermute x5, waiting for transfers between devices, swapped_sum(): lax.ppermute(value, axis, [(i, i ^ step) for i in range(size)])  13.8 us
    all_to_all x1, starting transfers between devices, per_device(): lax.all_to_all(everyone, 'seq', split_axis=0, concat_axis=0, tiled=True)  12 us
    pallas_call x5, Pallas kernels, call(): pl.pallas_call(kernel, out_shape=[jax.ShapeDtypeStruct(shape, dtype) for...  11.6 us
    unnamed x52, local copies, waits for them, and re-layouts  11.6 us
    all_to_all x1, waiting for transfers between devices, per_device(): lax.all_to_all(everyone, 'seq', split_axis=0, concat_axis=0, tiled=True)  11.4 us
  transfers between devices with their start and end apart: 8, of which 7 were waited for; matrix products, arithmetic and copies ran while one was open for 4% of the time, Pallas kernels for 5%

profile of v1, /device:TPU:10, one launch (start us, length us, event | category | flops | bytes accessed | tf_op | source)
XLA Modules:
  0.0 126.1 jit_solution(16996291629627253473)
XLA Ops:
  0.6 0.0 copy-start
  0.6 0.0 copy-start.4
  0.7 0.9 copy-done.4
  1.6 0.9 copy-done.6
  2.6 0.9 copy-done.8
  3.5 0.9 copy-done.17
  4.5 1.0 shard_map.163
  5.5 15.3 %all-to-all-start = ((bf16[16,128,128]{2,1,0:T(8,128)(2,1)}), bf16[16,128,128]{2,1,0:T(8,128)(2,1)S(1)}, u32[]{:S(2)}, u32[]{:S(2)}) async-start(bf16[16,128,128]{2,1,0:T(8,128)(2,1)} %shard_map.163), calls=%async_computation | async-start | bytes 1048576 | tf_op jit(solution)/shard_map/all_to_all | solution.py:314
  20.8 0.0 copy-done.24
  20.8 0.0 copy-start.3
  20.8 0.1 copy.19.rate_ref
  20.9 0.0 copy-done
  20.9 0.0 copy-done.10
  20.9 3.9 %cosine_bitcast_fusion = (f32[64,2048]{1,0:T(8,128)S(1)}, f32[64,2048]{1,0:T(8,128)S(1)}) fusion(f32[32,2048]{1,0:T(8,128)S(1)} %copy-done.10, f32[32,64]{1,0:T(8,128)S(1)} %copy-done), kind=kOutput, calls=%fused_computation | convolution fusion | flops 50331648 | bytes 1318912 | tf_op jit(solution)/shard_map/ej,et->jt/dot_general | solution.py:315
  24.9 0.0 copy-done.11
  24.9 0.0 copy-done.18
  24.9 0.0 copy-start.21
  24.9 0.7 copy-done.21
  25.6 1.6 %shard_map.164 = (f32[64,2048]{1,0:T(8,128)S(1)}, f32[64,2048]{1,0:T(8,128)S(1)}, f32[17,64,256]{2,1,0:T(8,128)S(1)}) custom-call(f32[64,2048]{1,0:T(8,128)S(1)} %get-tuple-element.25.hidden_ref, f32[64,64]{1,0:T(8,128)S(1)} %copy-done.18, f32[64,1]{1,0:T(8,128)S(1)} %copy.19.rate_ref, bf16[2,256,256]{2,1,0:T(8,128)(2,1)S(1)} %copy-done.11, ...), custom_call_target="tpu_custom_call" | custom-call | tf_op jit(solution)/shard_map/pallas_call | solution.py:288
  27.2 0.0 copy-start.13
  27.2 0.8 copy-done.13
  28.0 0.8 copy-done.15
  28.8 21.1 %all-to-all-done.got_ref = bf16[16,128,128]{2,1,0:T(8,128)(2,1)S(1)} async-done(((bf16[16,128,128]{2,1,0:T(8,128)(2,1)}), bf16[16,128,128]{2,1,0:T(8,128)(2,1)S(1)}, u32[]{:S(2)}, u32[]{:S(2)}) %all-to-all-start) | async-done | bytes 524320 | tf_op jit(solution)/shard_map/all_to_all | solution.py:314
  49.9 0.0 copy-done.3
  49.9 0.7 copy-done.19
  50.6 0.7 copy-done.22
  51.4 4.2 %shard_map.165 = (bf16[16,128,128]{2,1,0:T(8,128)(2,1)S(1)}, f32[17,64,256]{2,1,0:T(8,128)S(1)}) custom-call(bf16[16,128,128]{2,1,0:T(8,128)(2,1)S(1)} %all-to-all-done.got_ref, f32[17,64,256]{2,1,0:T(8,128)S(1)} %get-tuple-element.15.taps_ref, bf16[2,256,256]{2,1,0:T(8,128)(2,1)S(1)} %copy-done.11, bf16[2,256,256]{2,1,0:T(8,128)(2,1)S(1)} %copy-done.3, ...), custom_call_target="tpu_custom_call" | custom-call | tf_op jit(solution)/shard_map/pallas_call | solution.py:288
  55.5 0.0 copy-start.1
  55.5 1.0 copy-done.1
  56.5 0.8 copy-done.12
  57.3 6.4 %all-to-all-start.1 = ((bf16[16,128,128]{2,1,0:T(8,128)(2,1)}), bf16[16,128,128]{2,1,0:T(8,128)(2,1)S(1)}, u32[]{:S(2)}, u32[]{:S(2)}) async-start(bf16[16,128,128]{2,1,0:T(8,128)(2,1)} %copy-done.12), calls=%async_computation.1 | async-start | bytes 1048576 | tf_op jit(solution)/shard_map/all_to_all | solution.py:329
  63.8 0.0 copy-done.20
  63.8 0.0 copy-done.14
  63.8 0.0 copy-done.16
  63.8 0.0 copy-start.2
  63.8 1.2 copy-done.2
  65.0 3.7 %shard_map.167 = f32[64,128]{1,0:T(8,128)S(1)} custom-call(f32[17,64,256]{2,1,0:T(8,128)S(1)} %copy-done.2, f32[64,2048]{1,0:T(8,128)S(1)} %get-tuple-element.25.hidden_ref, f32[64,2048]{1,0:T(8,128)S(1)} %get-tuple-element.24.slope_ref, f32[32,2048]{1,0:T(8,128)S(1)} %copy-done.10, f32[64,64]{1,0:T(8,128)S(1)} %copy-done.18, f32[64,2048]{1,0:T(8,128)S(1)} %copy-done.14, ...), custom_call_target="tpu_custom_call" | custom-call | tf_op jit(solution)/shard_map/pallas_call | solution.py:288
  68.7 0.0 copy-start.9
  68.7 2.1 %collective-permute-start = (f32[64,128]{1,0:T(8,128)S(1)}, f32[64,128]{1,0:T(8,128)S(1)}, u32[]{:S(2)}, u32[]{:S(2)}) collective-permute-start(f32[64,128]{1,0:T(8,128)S(1)} %shard_map.167), channel_id=1, source_target_pairs={{0,128},{128,0},{256,384},{384,256},{1,129},{129,1},{257,385},{385... | collective-permute-start | bytes 98312 | tf_op jit(solution)/shard_map/ppermute | solution.py:300
  70.8 1.2 collective-permute-done
  72.0 4.2 %collective-permute-start.1 = (f32[64,128]{1,0:T(8,128)S(1)}, f32[64,128]{1,0:T(8,128)S(1)}, u32[]{:S(2)}, u32[]{:S(2)}) collective-permute-start(f32[64,128]{1,0:T(8,128)S(1)} %add.15), channel_id=1, source_target_pairs={{0,256},{128,384},{256,0},{384,128},{1,257},{129,385},{257,1},{385... | collective-permute-start | bytes 98312 | tf_op jit(solution)/shard_map/ppermute | solution.py:300
  76.2 3.1 %collective-permute-done.1 = f32[64,128]{1,0:T(8,128)S(1)} collective-permute-done((f32[64,128]{1,0:T(8,128)S(1)}, f32[64,128]{1,0:T(8,128)S(1)}, u32[]{:S(2)}, u32[]{:S(2)}) %collective-permute-start.1) | collective-permute-done | bytes 32800 | tf_op jit(solution)/shard_map/ppermute | solution.py:300
  79.3 0.1 slice.14
  79.4 2.3 %collective-permute-start.2 = (f32[32,64]{1,0:T(8,128)S(1)}, f32[32,64]{1,0:T(8,128)S(1)}, u32[]{:S(2)}, u32[]{:S(2)}) collective-permute-start(f32[32,64]{1,0:T(8,128)S(1)} %slice.14), channel_id=1, source_target_pairs={{0,16},{16,0},{32,48},{48,32},{64,80},{80,64},{96,112},{112,96},{1... | collective-permute-start | bytes 24584 | tf_op jit(solution)/shard_map/ppermute | solution.py:300
  81.7 3.3 %collective-permute-done.2 = f32[32,64]{1,0:T(8,128)S(1)} collective-permute-done((f32[32,64]{1,0:T(8,128)S(1)}, f32[32,64]{1,0:T(8,128)S(1)}, u32[]{:S(2)}, u32[]{:S(2)}) %collective-permute-start.2) | collective-permute-done | bytes 8224 | tf_op jit(solution)/shard_map/ppermute | solution.py:300
  85.0 0.1 slice_add_fusion
  85.1 2.4 %collective-permute-start.3 = (f32[32,64]{1,0:T(8,128)S(1)}, f32[32,64]{1,0:T(8,128)S(1)}, u32[]{:S(2)}, u32[]{:S(2)}) collective-permute-start(f32[32,64]{1,0:T(8,128)S(1)} %slice_add_fusion), channel_id=1, source_target_pairs={{0,32},{16,48},{32,0},{48,16},{64,96},{80,112},{96,64},{112,80},{1... | collective-permute-start | bytes 24584 | tf_op jit(solution)/shard_map/ppermute | solution.py:300
  87.5 3.2 %collective-permute-done.3 = f32[32,64]{1,0:T(8,128)S(1)} collective-permute-done((f32[32,64]{1,0:T(8,128)S(1)}, f32[32,64]{1,0:T(8,128)S(1)}, u32[]{:S(2)}, u32[]{:S(2)}) %collective-permute-start.3) | collective-permute-done | bytes 8224 | tf_op jit(solution)/shard_map/ppermute | solution.py:300
  90.7 4.0 %collective-permute-start.4 = (f32[32,64]{1,0:T(8,128)S(1)}, f32[32,64]{1,0:T(8,128)S(1)}, u32[]{:S(2)}, u32[]{:S(2)}) collective-permute-start(f32[32,64]{1,0:T(8,128)S(1)} %add.18), channel_id=1, source_target_pairs={{0,64},{16,80},{32,96},{48,112},{64,0},{80,16},{96,32},{112,48},{1... | collective-permute-start | bytes 24584 | tf_op jit(solution)/shard_map/ppermute | solution.py:300
  94.7 3.1 %collective-permute-done.4 = f32[32,64]{1,0:T(8,128)S(1)} collective-permute-done((f32[32,64]{1,0:T(8,128)S(1)}, f32[32,64]{1,0:T(8,128)S(1)}, u32[]{:S(2)}, u32[]{:S(2)}) %collective-permute-start.4) | collective-permute-done | bytes 8224 | tf_op jit(solution)/shard_map/ppermute | solution.py:300
  97.8 0.0 all-to-all-done.1.got_ref
  97.8 0.8 reshape.13
  98.7 12.0 %all-to-all-start.2 = ((f32[16,1,2048]{2,1,0:T(1,128)}), f32[16,1,2048]{2,1,0:T(1,128)S(1)}, u32[]{:S(2)}, u32[]{:S(2)}) async-start(f32[16,1,2048]{2,1,0:T(1,128)} %reshape.13), calls=%async_computation.2 | async-start | bytes 262144 | tf_op jit(solution)/shard_map/all_to_all | solution.py:348
  110.7 0.6 slice_bitcast_fusion
  111.3 0.0 copy-done.5
  111.3 0.0 copy-done.7
  111.3 0.0 copy-done.9
  111.3 1.1 shard_map.166
  112.4 0.0 copy-done.23
  112.4 11.4 %all-to-all-done.2 = f32[16,1,2048]{2,1,0:T(1,128)S(1)} async-done(((f32[16,1,2048]{2,1,0:T(1,128)}), f32[16,1,2048]{2,1,0:T(1,128)S(1)}, u32[]{:S(2)}, u32[]{:S(2)}) %all-to-all-start.2) | async-done | bytes 131104 | tf_op jit(solution)/shard_map/all_to_all | solution.py:348
  123.8 0.5 broadcast.1
  124.4 0.9 reduce
  125.3 0.1 reshape.14
  125.4 0.6 reduce_sum.9
  (22 shorter events, 0.1 us)
Async XLA Ops:
  0.6 20.3 %copy-start = (f32[32,64]{1,0:T(8,128)S(1)}, f32[32,64]{1,0:T(8,128)}, u32[]{:S(2)}) copy-start(f32[32,64]{1,0:T(8,128)} %param.16) | copy-start | bytes 24580
  0.6 1.0 copy-start.4
  1.6 0.9 copy-start.6
  2.6 0.9 copy-start.8
  3.5 0.9 copy-start.17
  4.5 16.4 %copy-start.24 = (f32[64]{0:T(128)S(1)}, f32[64]{0:T(128)}, u32[]{:S(2)}) copy-start(f32[64]{0:T(128)} %param.18) | copy-start | bytes 772
  4.5 16.5 %copy-start.10 = (f32[32,2048]{1,0:T(8,128)S(1)}, f32[32,2048]{1,0:T(8,128)}, u32[]{:S(2)}) copy-start(f32[32,2048]{1,0:T(8,128)} %constant.16.clone.features_ref) | copy-start | bytes 786436
  5.5 19.4 %copy-start.11 = (bf16[2,256,256]{2,1,0:T(8,128)(2,1)S(1)}, bf16[2,256,256]{2,1,0:T(8,128)(2,1)}, u32[]{:S(2)}) copy-start(bf16[2,256,256]{2,1,0:T(8,128)(2,1)} %constant.12.clone.table_ref) | copy-start | bytes 786436
  5.5 19.4 %copy-start.18 = (f32[64,64]{1,0:T(8,128)S(1)}, f32[64,64]{1,0:T(8,128)}, u32[]{:S(2)}) copy-start(f32[64,64]{1,0:T(8,128)} %filter_ref.3) | copy-start | bytes 49156
  5.5 44.4 %all-to-all-start = ((bf16[16,128,128]{2,1,0:T(8,128)(2,1)}), bf16[16,128,128]{2,1,0:T(8,128)(2,1)S(1)}, u32[]{:S(2)}, u32[]{:S(2)}) async-start(bf16[16,128,128]{2,1,0:T(8,128)(2,1)} %shard_map.163), calls=%async_computation | async-start | bytes 1048576 | tf_op jit(solution)/shard_map/all_to_all | solution.py:314
  20.8 29.1 %copy-start.3 = (bf16[2,256,256]{2,1,0:T(8,128)(2,1)S(1)}, bf16[2,256,256]{2,1,0:T(8,128)(2,1)}, u32[]{:S(2)}) copy-start(bf16[2,256,256]{2,1,0:T(8,128)(2,1)} %constant.13.clone.back_table_ref) | copy-start | bytes 786436
  24.9 0.7 copy-start.21
  27.2 0.8 copy-start.13
  28.0 0.8 copy-start.15
  49.9 0.7 copy-start.19
  50.6 0.7 copy-start.22
  51.3 12.4 %copy-start.20 = (f32[17,2,128]{2,1,0:T(2,128)S(1)}, f32[17,2,128]{2,1,0:T(2,128)}, u32[]{:S(2)}) copy-start(f32[17,2,128]{2,1,0:T(2,128)} %constant.15.clone.untwist_ref) | copy-start | bytes 52228
  55.5 1.0 copy-start.1
  56.5 0.8 copy-start.12
  57.3 6.5 %copy-start.14 = (f32[64,2048]{1,0:T(8,128)S(1)}, f32[64,2048]{1,0:T(8,128)}, u32[]{:S(2)}) copy-start(f32[64,2048]{1,0:T(8,128)} %copy-done.13) | copy-start | bytes 1572868
  57.3 6.5 %copy-start.16 = (f32[64,2048]{1,0:T(8,128)S(1)}, f32[64,2048]{1,0:T(8,128)}, u32[]{:S(2)}) copy-start(f32[64,2048]{1,0:T(8,128)} %copy-done.15) | copy-start | bytes 1572868
  57.3 40.5 %all-to-all-start.1 = ((bf16[16,128,128]{2,1,0:T(8,128)(2,1)}), bf16[16,128,128]{2,1,0:T(8,128)(2,1)S(1)}, u32[]{:S(2)}, u32[]{:S(2)}) async-start(bf16[16,128,128]{2,1,0:T(8,128)(2,1)} %copy-done.12), calls=%async_computation.1 | async-start | bytes 1048576 | tf_op jit(solution)/shard_map/all_to_all | solution.py:329
  63.8 1.2 copy-start.2
  68.7 42.6 %copy-start.5 = (bf16[1,128,1024]{2,1,0:T(8,128)(2,1)S(1)}, bf16[1,128,1024]{2,1,0:T(8,128)(2,1)}, u32[]{:S(2)}) copy-start(bf16[1,128,1024]{2,1,0:T(8,128)(2,1)} %key_ref.3) | copy-start | bytes 786436
  68.7 42.6 %copy-start.7 = (bf16[1,128,1024]{2,1,0:T(8,128)(2,1)S(1)}, bf16[1,128,1024]{2,1,0:T(8,128)(2,1)}, u32[]{:S(2)}) copy-start(bf16[1,128,1024]{2,1,0:T(8,128)(2,1)} %value_ref.3) | copy-start | bytes 786436
  68.7 42.6 %copy-start.9 = (bf16[1,128,1024]{2,1,0:T(8,128)(2,1)S(1)}, bf16[1,128,1024]{2,1,0:T(8,128)(2,1)}, u32[]{:S(2)}) copy-start(bf16[1,128,1024]{2,1,0:T(8,128)(2,1)} %grad_ref.3) | copy-start | bytes 786436
  68.7 3.2 %collective-permute-start = (f32[64,128]{1,0:T(8,128)S(1)}, f32[64,128]{1,0:T(8,128)S(1)}, u32[]{:S(2)}, u32[]{:S(2)}) collective-permute-start(f32[64,128]{1,0:T(8,128)S(1)} %shard_map.167), channel_id=1, source_target_pairs={{0,128},{128,0},{256,384},{384,256},{1,129},{129,1},{257,385},{385... | collective-permute-start | bytes 98312 | tf_op jit(solution)/shard_map/ppermute | solution.py:300
  72.0 7.3 %collective-permute-start.1 = (f32[64,128]{1,0:T(8,128)S(1)}, f32[64,128]{1,0:T(8,128)S(1)}, u32[]{:S(2)}, u32[]{:S(2)}) collective-permute-start(f32[64,128]{1,0:T(8,128)S(1)} %add.15), channel_id=1, source_target_pairs={{0,256},{128,384},{256,0},{384,128},{1,257},{129,385},{257,1},{385... | collective-permute-start | bytes 98312 | tf_op jit(solution)/shard_map/ppermute | solution.py:300
  79.3 33.2 %copy-start.23 = (f32[64,128]{1,0:T(8,128)}, f32[64,128]{1,0:T(8,128)S(1)}, u32[]{:S(2)}) copy-start(f32[64,128]{1,0:T(8,128)S(1)} %add.16) | copy-start | bytes 98308
  79.4 5.6 %collective-permute-start.2 = (f32[32,64]{1,0:T(8,128)S(1)}, f32[32,64]{1,0:T(8,128)S(1)}, u32[]{:S(2)}, u32[]{:S(2)}) collective-permute-start(f32[32,64]{1,0:T(8,128)S(1)} %slice.14), channel_id=1, source_target_pairs={{0,16},{16,0},{32,48},{48,32},{64,80},{80,64},{96,112},{112,96},{1... | collective-permute-start | bytes 24584 | tf_op jit(solution)/shard_map/ppermute | solution.py:300
  85.1 5.6 %collective-permute-start.3 = (f32[32,64]{1,0:T(8,128)S(1)}, f32[32,64]{1,0:T(8,128)S(1)}, u32[]{:S(2)}, u32[]{:S(2)}) collective-permute-start(f32[32,64]{1,0:T(8,128)S(1)} %slice_add_fusion), channel_id=1, source_target_pairs={{0,32},{16,48},{32,0},{48,16},{64,96},{80,112},{96,64},{112,80},{1... | collective-permute-start | bytes 24584 | tf_op jit(solution)/shard_map/ppermute | solution.py:300
  90.7 7.1 %collective-permute-start.4 = (f32[32,64]{1,0:T(8,128)S(1)}, f32[32,64]{1,0:T(8,128)S(1)}, u32[]{:S(2)}, u32[]{:S(2)}) collective-permute-start(f32[32,64]{1,0:T(8,128)S(1)} %add.18), channel_id=1, source_target_pairs={{0,64},{16,80},{32,96},{48,112},{64,0},{80,16},{96,32},{112,48},{1... | collective-permute-start | bytes 24584 | tf_op jit(solution)/shard_map/ppermute | solution.py:300
  98.7 25.2 %all-to-all-start.2 = ((f32[16,1,2048]{2,1,0:T(1,128)}), f32[16,1,2048]{2,1,0:T(1,128)S(1)}, u32[]{:S(2)}, u32[]{:S(2)}) async-start(f32[16,1,2048]{2,1,0:T(1,128)} %reshape.13), calls=%async_computation.2 | async-start | bytes 262144 | tf_op jit(solution)/shard_map/all_to_all | solution.py:348

commit v2 on v1

v2 whole, which is shorter than its diff:
```python
import math

import jax
import jax.numpy as jnp
import numpy as np
from jax import lax
from jax.experimental import pallas as pl
from jax.experimental.pallas import tpu as pltpu
from jax.sharding import PartitionSpec as P

BLOCKS = 16
INNER = 128
GROUP = 64
HALF = 17
LENGTH = BLOCKS * INNER
PERIOD = 2 * LENGTH
VMEM = pl.BlockSpec(memory_space=pltpu.VMEM)
HBM = pl.BlockSpec(memory_space=pltpu.HBM)


def split_table(table):
    high = table.astype(jnp.bfloat16)
    low = (table - high.astype(np.float64)).astype(jnp.bfloat16)
    return np.stack([high, low])


def tables():
    inner = np.arange(INNER)
    angle = 2.0 * math.pi * (np.outer(inner, inner) % INNER) / INNER
    cos, sin = np.cos(angle), np.sin(angle)
    forward = np.block([[cos, -sin], [sin, cos]])
    turn = 2.0 * math.pi * np.outer(np.arange(HALF), inner) / PERIOD
    weight = np.full((HALF, 1), 2.0 / PERIOD)
    weight[0] = weight[-1] = 1.0 / PERIOD
    turns = np.zeros((4, 24, INNER), np.float32)
    for i, part in enumerate((np.cos(turn), np.sin(turn), np.cos(turn) * weight, np.sin(turn) * weight)):
        turns[i, :HALF] = part
    return split_table(forward), turns


def embed_features(count):
    bands = np.arange(count // 2) + 0.5
    phase = np.arange(LENGTH)[None, :] * bands[:, None] * (2.0 * math.pi / LENGTH)
    return np.concatenate([np.sin(phase), np.cos(phase)], axis=0).astype(np.float32)


def weighted_sum(terms):
    total = None
    for value, factor in terms:
        if abs(factor) < 1e-9:
            continue
        if abs(factor - 1.0) < 1e-9:
            total = value if total is None else total + value
        elif abs(factor + 1.0) < 1e-9:
            total = -value if total is None else total - value
        else:
            part = value * np.float32(factor)
            total = part if total is None else total + part
    return total


def odd_bins(x):
    size = len(x)
    half = size // 2
    if size == 2:
        return {1: (x[0], -x[1])}
    minus = {n: x[n] - x[size - n] for n in range(1, half)}
    plus = {n: x[n] + x[size - n] for n in range(1, half)}
    minus[0] = x[0]
    plus[half] = x[half]
    out = {}
    for k in range(1, half, 2):
        cos = lambda n: math.cos(math.pi * k * n / size)
        sin = lambda n: math.sin(math.pi * k * n / size)
        cos_even = weighted_sum([(minus[n], cos(n)) for n in range(0, half, 2)])
        cos_odd = weighted_sum([(minus[n], cos(n)) for n in range(1, half, 2)])
        sin_even = weighted_sum([(plus[n], sin(n)) for n in range(2, half + 1, 2)])
        sin_odd = weighted_sum([(plus[n], sin(n)) for n in range(1, half, 2)])
        out[k] = (cos_even + cos_odd, -(sin_even + sin_odd))
        out[size - k] = (cos_even - cos_odd, sin_even - sin_odd)
    return out


def real_bins(x):
    size = len(x)
    half = size // 2
    if size == 2:
        return {0: (x[0] + x[1], None), 1: (x[0] - x[1], None)}
    out = {2 * k: v for k, v in real_bins([x[n] + x[n + half] for n in range(half)]).items()}
    out.update(odd_bins([x[n] - x[n + half] for n in range(half)]))
    return out


def outer_bins(x):
    out = {2 * k: v for k, v in real_bins(x).items()}
    out.update(odd_bins(x))
    return out


def odd_times(bins, size):
    half = size // 2
    if size == 2:
        return [bins[1][0], -bins[1][1]]
    ks = range(1, half, 2)
    real_plus = {k: bins[k][0] + bins[size - k][0] for k in ks}
    real_minus = {k: bins[k][0] - bins[size - k][0] for k in ks}
    imag_plus = {k: bins[k][1] + bins[size - k][1] for k in ks}
    imag_minus = {k: bins[k][1] - bins[size - k][1] for k in ks}
    out = [None] * size
    for n in range(half + 1):
        reals, imags = (real_minus, imag_plus) if n % 2 else (real_plus, imag_minus)
        cos = weighted_sum([(reals[k], math.cos(math.pi * k * n / size)) for k in ks])
        sin = weighted_sum([(imags[k], math.sin(math.pi * k * n / size)) for k in ks])
        if n == 0:
            out[0] = cos
        elif n == half:
            out[half] = -sin
        else:
            out[n] = cos - sin
            out[size - n] = -(cos + sin)
    return out


def real_times(bins, size):
    if size == 2:
        return [bins[0][0] + bins[1][0], bins[0][0] - bins[1][0]]
    half = size // 2
    even = real_times({k // 2: v for k, v in bins.items() if k % 2 == 0}, half)
    odd = odd_times({k: v for k, v in bins.items() if k % 2}, half)
    return [even[n] + odd[n] for n in range(half)] + [even[n] - odd[n] for n in range(half)]


def outer_times(bins, size):
    even = real_times({k // 2: v for k, v in bins.items() if k % 2 == 0}, size)
    odd = odd_times({k: v for k, v in bins.items() if k % 2}, size)
    return [even[n] + odd[n] for n in range(size)]


def split(values):
    high = values.astype(jnp.bfloat16)
    return high, (values - high.astype(jnp.float32)).astype(jnp.bfloat16)


def precise_dot(values, table_ref, side=0):
    high, low = split(values)
    dims = (((1,), (side,)), ((), ()))
    dot = lambda a, b: lax.dot_general(a, b, dims, preferred_element_type=jnp.float32)
    return dot(high, table_ref[0]) + (dot(low, table_ref[0]) + dot(high, table_ref[1]))


def forward_outer(load, rows, turns_ref, turned_ref):
    @pl.loop(0, rows // 8)
    def _(step):
        where = pl.ds(pl.multiple_of(step * 8, 8), 8)
        bins = outer_bins([load(n, where) for n in range(BLOCKS)])
        for k in range(HALF):
            real, imag = bins[k]
            cos, sin = turns_ref[0, k : k + 1, :], turns_ref[1, k : k + 1, :]
            if k == 0:
                turned_real, turned_imag = real, jnp.zeros_like(real)
            elif imag is None:
                turned_real, turned_imag = real * cos, -real * sin
            else:
                turned_real, turned_imag = real * cos + imag * sin, imag * cos - real * sin
            turned_ref[k, where, :INNER] = turned_real
            turned_ref[k, where, INNER:] = turned_imag


def inverse_outer(back_ref, offset, rows, turns_ref, store):
    @pl.loop(0, rows // 8)
    def _(step):
        where = pl.ds(pl.multiple_of(step * 8, 8), 8)
        place = pl.ds(pl.multiple_of(offset + step * 8, 8), 8)
        bins = {}
        for k in range(HALF):
            real, imag = back_ref[k, place, :INNER], back_ref[k, place, INNER:]
            cos, sin = turns_ref[2, k : k + 1, :], turns_ref[3, k : k + 1, :]
            if k in (0, HALF - 1):
                bins[k] = (real * cos - imag * sin, None)
            else:
                bins[k] = (real * cos - imag * sin, real * sin + imag * cos)
        for n, value in enumerate(outer_times(bins, BLOCKS)):
            store(n, where, value)


def pack_kernel(
    query_hbm, key_hbm, value_hbm, grad_hbm, sent_hbm, key_ref, value_ref, grad_ref, query_ref, sent_ref, sems, out_sems
):
    pairs = ((key_hbm, key_ref), (value_hbm, value_ref), (grad_hbm, grad_ref), (query_hbm, query_ref))
    copies = []
    for i, (source, target) in enumerate(pairs):
        for half in range(2):
            rows = pl.ds(half * (INNER // 2), INNER // 2)
            copies.append(pltpu.make_async_copy(source.at[0, rows], target.at[rows], sems.at[2 * i + half]))
            copies[-1].start()
    outs = []
    for part, (first, second) in enumerate(((key_ref, value_ref), (grad_ref, query_ref))):
        place = part * GROUP
        for copy in copies[4 * part : 4 * part + 4]:
            copy.wait()
        for pair in range(BLOCKS // 2):
            lanes = slice(2 * GROUP * pair, 2 * GROUP * (pair + 1))
            both = first[:, lanes].astype(jnp.float32) * second[:, lanes].astype(jnp.float32)
            both = both.T.astype(jnp.bfloat16)
            sent_ref[2 * pair, place : place + GROUP] = both[:GROUP]
            sent_ref[2 * pair + 1, place : place + GROUP] = both[GROUP:]
            if part == 1 and pair % 2 == 1:
                where = pl.ds(2 * (pair - 1), 4)
                outs.append(pltpu.make_async_copy(sent_ref.at[where], sent_hbm.at[where], out_sems.at[pair // 2]))
                outs[-1].start()
    for copy in outs:
        copy.wait()


def decay_window(params_ref):
    positions = lax.broadcasted_iota(jnp.int32, (1, LENGTH), 1).astype(jnp.float32)
    return jnp.exp(-params_ref[:, GROUP : GROUP + 1] * positions / LENGTH)


def filter_kernel(hidden_ref, params_ref, table_ref, turns_ref, spec_ref, taps_ref, turned_ref):
    taps_ref[...] = decay_window(params_ref) * lax.dot_general(
        params_ref[:, :GROUP],
        hidden_ref[...],
        (((0,), (0,)), ((), ())),
        precision=lax.Precision.HIGHEST,
        preferred_element_type=jnp.float32,
    )
    forward_outer(
        lambda n, where: taps_ref[where, n * INNER : (n + 1) * INNER], GROUP, turns_ref, turned_ref
    )
    turned = turned_ref[...].reshape(HALF * GROUP, 2 * INNER)
    spec_ref[...] = precise_dot(turned, table_ref).reshape(HALF, GROUP, 2 * INNER)


def precise(a, b, dims):
    (a_high, a_low), (b_high, b_low) = split(a), split(b)
    dot = lambda x, y: lax.dot_general(x, y, (dims, ((), ())), preferred_element_type=jnp.float32)
    return dot(a_high, b_high) + (dot(a_low, b_high) + dot(a_high, b_low))


def spectra(turned_ref, table_ref, first, last):
    count = last - first
    turned = turned_ref[first:last].reshape(count * 2 * GROUP, 2 * INNER)
    spec = precise_dot(turned, table_ref).reshape(count, 2 * GROUP, 2 * INNER)
    in_real, in_imag = spec[:, :GROUP, :INNER], spec[:, :GROUP, INNER:]
    up_real, up_imag = spec[:, GROUP:, :INNER], spec[:, GROUP:, INNER:]
    corr = pair(in_real * up_real + in_imag * up_imag, in_real * up_imag - in_imag * up_real)
    return in_real, in_imag, up_real, up_imag, corr


def pair(real, imag):
    return jnp.concatenate([real, imag], axis=2)


def forward_both(got_ref, wide_ref, turns_ref, turned_ref):
    wide_ref[...] = got_ref[...].astype(jnp.float32)
    forward_outer(lambda n, where: wide_ref[n, where, :], 2 * GROUP, turns_ref, turned_ref)


def weighted_corr(back_ref, offset, params_ref, turns_ref, corr_time_ref):
    def store(n, where, value):
        corr_time_ref[where, n * INNER : (n + 1) * INNER] = value * np.float32(1.0 / math.sqrt(4 * LENGTH))

    inverse_outer(back_ref, offset, GROUP, turns_ref, store)
    return corr_time_ref[...] * decay_window(params_ref)


PARTS = ((0, 4), (4, 8), (8, 12), (12, HALF))
ALONG = ((1,), (1,))
TIME_SCALE = np.float32(1.0 / math.sqrt(LENGTH))


def embed_kernel(
    got_ref, slope_ref, features_ref, params_ref, table_ref, turns_ref, share_ref, wide_ref, turned_ref, back_ref, corr_time_ref
):
    forward_both(got_ref, wide_ref, turns_ref, turned_ref)
    for first, last in PARTS:
        corr = spectra(turned_ref, table_ref, first, last)[4]
        back = precise_dot(corr.reshape((last - first) * GROUP, 2 * INNER), table_ref, 1)
        back_ref[first:last] = back.reshape(last - first, GROUP, 2 * INNER)
    weighted = weighted_corr(back_ref, 0, params_ref, turns_ref, corr_time_ref)
    hidden_grad = precise(params_ref[:, :GROUP], weighted, ((1,), (0,))) * slope_ref[...]
    embed = precise(features_ref[...], hidden_grad, ALONG) * TIME_SCALE
    embed = jnp.concatenate([embed[:16], embed[16:]], axis=1).astype(jnp.bfloat16)
    share_ref[...] = jnp.broadcast_to(embed[None], share_ref.shape)


def main_kernel(
    got_ref, taps_ref, hidden_ref, params_ref, table_ref, turns_ref, out_ref, grads_ref, wide_ref, turned_ref, back_ref, corr_time_ref
):
    forward_both(got_ref, wide_ref, turns_ref, turned_ref)
    for first, last in PARTS:
        in_real, in_imag, up_real, up_imag, corr = spectra(turned_ref, table_ref, first, last)
        tap_real, tap_imag = taps_ref[first:last, :, :INNER], taps_ref[first:last, :, INNER:]
        conv = pair(tap_real * in_real - tap_imag * in_imag, tap_real * in_imag + tap_imag * in_real)
        grad = pair(tap_real * up_real + tap_imag * up_imag, tap_real * up_imag - tap_imag * up_real)
        joined = jnp.concatenate([conv, grad, corr], axis=1)
        back = precise_dot(joined.reshape((last - first) * 3 * GROUP, 2 * INNER), table_ref, 1)
        back_ref[first:last] = back.reshape(last - first, 3 * GROUP, 2 * INNER)

    def store(n, where, value):
        wide_ref[n, where, :] = value

    inverse_outer(back_ref, 0, 2 * GROUP, turns_ref, store)
    for n in range(BLOCKS):
        out_ref[n, : 2 * GROUP] = wide_ref[n].astype(jnp.bfloat16)
        out_ref[n, 2 * GROUP :] = jnp.zeros((16, INNER), jnp.bfloat16)
    weighted = weighted_corr(back_ref, 2 * GROUP, params_ref, turns_ref, corr_time_ref)
    grads_ref[:, :GROUP] = precise(hidden_ref[...], weighted, ALONG) * TIME_SCALE
    slopes = weighted * precise(params_ref[:, :GROUP], hidden_ref[...], ((0,), (0,)))
    inner = lax.broadcasted_iota(jnp.int32, (1, INNER), 1)
    rate = jnp.zeros((GROUP, INNER), jnp.float32)
    for n in range(BLOCKS):
        positions = (inner + n * INNER).astype(jnp.float32) / LENGTH
        rate += positions * slopes[:, n * INNER : (n + 1) * INNER]
    grads_ref[:, GROUP:] = precise(jnp.full((GROUP, INNER), -1.0, jnp.float32), rate, ALONG) * TIME_SCALE


def insert_kernel(shares_ref, _, out_hbm, total_ref, sems):
    total_ref[...] = jnp.sum(shares_ref[...].astype(jnp.float32), axis=0).astype(jnp.bfloat16)
    copies = []
    for n in range(BLOCKS):
        target = out_hbm.at[n, pl.ds(2 * GROUP, 16)]
        copies.append(pltpu.make_async_copy(total_ref, target, sems.at[n]))
        copies[-1].start()
    for copy in copies:
        copy.wait()


def apply_kernel(got_ref, key_ref, value_ref, grad_ref, d_query_ref, d_key_ref, d_value_ref, embed_ref):
    total = jnp.sum(got_ref[:, 2 * GROUP :, :].astype(jnp.float32), axis=0)
    embed_ref[:16] = total[:, :GROUP]
    embed_ref[16:] = total[:, GROUP:]
    for pair in range(BLOCKS // 2):
        lanes = slice(2 * GROUP * pair, 2 * GROUP * (pair + 1))

        def times(place):
            both = [got_ref[2 * pair + i, place : place + GROUP].astype(jnp.float32) for i in (0, 1)]
            return jnp.concatenate(both, axis=0).T

        conv, grad = times(0), times(GROUP)
        d_query_ref[0, :, lanes] = (grad_ref[0, :, lanes].astype(jnp.float32) * conv).astype(jnp.bfloat16)
        d_key_ref[0, :, lanes] = (grad * value_ref[0, :, lanes].astype(jnp.float32)).astype(jnp.bfloat16)
        d_value_ref[0, :, lanes] = (grad * key_ref[0, :, lanes].astype(jnp.float32)).astype(jnp.bfloat16)


def call(kernel, outs, ins, scratch=(), in_specs=None, out_specs=None, aliases=(), megabytes=8):
    return pl.pallas_call(
        kernel,
        out_shape=[jax.ShapeDtypeStruct(shape, dtype) for shape, dtype in outs],
        in_specs=in_specs or [VMEM] * len(ins),
        out_specs=out_specs or [VMEM] * len(outs),
        scratch_shapes=list(scratch),
        input_output_aliases=dict(aliases),
        compiler_params=pltpu.CompilerParams(vmem_limit_bytes=megabytes * 1024 * 1024),
    )(*ins)


def swapped_sum(value, axis, step):
    size = lax.axis_size(axis)
    return value + lax.ppermute(value, axis, [(i, i ^ step) for i in range(size)])


def per_device(query_input, key_input, value_input, grad_output, w_embed, w_filter, decay_rates):
    f32, bf16 = jnp.float32, jnp.bfloat16
    forward, turns = (jnp.asarray(t) for t in tables())
    features = jnp.asarray(embed_features(w_embed.shape[0]))
    spectrum = (HALF, GROUP, 2 * INNER)
    piece = (INNER, query_input.shape[2])
    moved = (BLOCKS, 2 * GROUP, INNER)
    loaded = (BLOCKS, 2 * GROUP + 16, INNER)
    flat = (GROUP, LENGTH)
    (sent,) = call(
        pack_kernel,
        [(moved, bf16)],
        (query_input, key_input, value_input, grad_output),
        [pltpu.VMEM(piece, bf16)] * 4
        + [pltpu.VMEM(moved, bf16), pltpu.SemaphoreType.DMA((8,)), pltpu.SemaphoreType.DMA((4,))],
        in_specs=[HBM] * 4,
        out_specs=[HBM],
        megabytes=58,
    )
    got = lax.all_to_all(sent, "seq", split_axis=0, concat_axis=0, tiled=True)
    pre = jnp.einsum("ej,et->jt", w_embed, features, precision=lax.Precision.HIGHEST)
    hidden, slope = jnp.sin(pre), jnp.cos(pre)
    params = jnp.concatenate(
        [w_filter, jnp.broadcast_to(decay_rates[:, None], (GROUP, INNER - GROUP))], axis=1
    )
    (taps_spec,) = call(
        filter_kernel,
        [(spectrum, f32)],
        (hidden, params, forward, turns),
        [pltpu.VMEM(flat, f32), pltpu.VMEM(spectrum, f32)],
        megabytes=16,
    )
    plane = ("dp", "chan")
    both = (HALF, 2 * GROUP, 2 * INNER)
    got, taps_spec = lax.optimization_barrier((got, taps_spec))
    (shares,) = call(
        embed_kernel,
        [((lax.axis_size(plane), 16, INNER), bf16)],
        (got, slope, features, params, forward, turns),
        [pltpu.VMEM(moved, f32), pltpu.VMEM(both, f32), pltpu.VMEM(spectrum, f32), pltpu.VMEM(flat, f32)],
        megabytes=24,
    )
    shares = lax.all_to_all(shares, plane, split_axis=0, concat_axis=0, tiled=True)
    result, grads = call(
        main_kernel,
        [(loaded, bf16), ((GROUP, 2 * GROUP), f32)],
        (got, taps_spec, hidden, params, forward, turns),
        [
            pltpu.VMEM(moved, f32),
            pltpu.VMEM(both, f32),
            pltpu.VMEM((HALF, 3 * GROUP, 2 * INNER), f32),
            pltpu.VMEM(flat, f32),
        ],
        megabytes=28,
    )
    (result,) = call(
        insert_kernel,
        [(loaded, bf16)],
        (shares, result),
        [pltpu.VMEM((16, INNER), bf16), pltpu.SemaphoreType.DMA((BLOCKS,))],
        in_specs=[VMEM, HBM],
        out_specs=[HBM],
        aliases=((1, 0),),
        megabytes=58,
    )
    result, grads = lax.optimization_barrier((result, grads))
    back = lax.all_to_all(result, "seq", split_axis=0, concat_axis=0, tiled=True)
    grads = swapped_sum(swapped_sum(grads, "dp", 1), "dp", 2)
    d_query, d_key, d_value, grad_embed = call(
        apply_kernel,
        [(query_input.shape, bf16)] * 3 + [(w_embed.shape, f32)],
        (back, key_input, value_input, grad_output),
        megabytes=12,
    )
    return (d_query, d_key, d_value, grads[:, :GROUP], grads[0, GROUP:], grad_embed)


def solution(mesh):
    wide = P("dp", "seq", "chan")
    split = ("chan", "seq")
    return jax.shard_map(
        per_device,
        mesh=mesh,
        in_specs=(wide, wide, wide, wide, P(), P(None, split), P(split)),
        out_specs=(wide, wide, wide, P(None, split), P(split), P()),
        check_vma=False,
    )
```

time: 127 us -> 111 us (0.87)
  the two profiles are of different devices: /device:TPU:10 before, /device:TPU:32 now
where the time goes in v2:
time: 111 us; the launch traced here: 110 us
  waiting for transfers between devices  47.3 us (43%)
  starting transfers between devices  36.6 us (33%)
  Pallas kernels  19.4 us (17%)
  matrix products  3.92 us (4%)
  local copies, waits for them, and re-layouts  2.2 us (2%)
    all_to_all x1, waiting for transfers between devices, per_device(): got = lax.all_to_all(sent, 'seq', split_axis=0, concat_axis=0, tiled=True)  22.5 us
    all_to_all x1, waiting for transfers between devices, per_device(): lax.all_to_all(result, 'seq', split_axis=0, concat_axis=0, tiled=True)  20.8 us
    pallas_call x6, Pallas kernels, call(): pl.pallas_call(kernel, out_shape=[jax.ShapeDtypeStruct(shape, dtype) for...  19.4 us
    all_to_all x1, starting transfers between devices, per_device(): got = lax.all_to_all(sent, 'seq', split_axis=0, concat_axis=0, tiled=True)  15.4 us
    all_to_all x1, starting transfers between devices, per_device(): lax.all_to_all(shares, plane, split_axis=0, concat_axis=0, tiled=True)  7.32 us
    all_to_all x1, starting transfers between devices, per_device(): lax.all_to_all(result, 'seq', split_axis=0, concat_axis=0, tiled=True)  7.17 us
    ppermute x2, starting transfers between devices, swapped_sum(): lax.ppermute(value, axis, [(i, i ^ step) for i in range(size)])  6.77 us
    dot_general x1, matrix products, per_device(): jnp.einsum('ej,et->jt', w_embed, features, precision=lax.Precision.HIGHEST)  3.92 us
  transfers between devices with their start and end apart: 5, of which 5 were waited for; matrix products, arithmetic and copies ran while one was open for 4% of the time, Pallas kernels for 7%

profile of v2, /device:TPU:32, one launch (start us, length us, event | category | flops | bytes accessed | tf_op | source)
XLA Modules:
  0.0 110.3 jit_solution(16871401334540273896)
XLA Ops:
  0.6 0.0 copy-start
  0.6 0.0 copy-start.3
  0.7 0.0 copy-start.9
  0.7 0.0 copy-start.11
  0.7 2.3 %shard_map.145 = bf16[16,128,128]{2,1,0:T(8,128)(2,1)} custom-call(bf16[1,128,1024]{2,1,0:T(8,128)(2,1)} %query_hbm.1, bf16[1,128,1024]{2,1,0:T(8,128)(2,1)} %key_ref.1, bf16[1,128,1024]{2,1,0:T(8,128)(2,1)} %value_ref.1, bf16[1,128,1024]{2,1,0:T(8,128)(2,1)} %grad_ref.1), custom_call_target="tpu_custom_call" | custom-call | tf_op jit(solution)/shard_map/pallas_call | solution.py:348
  3.0 0.0 copy-start.1
  3.0 0.0 copy-start.7
  3.1 15.4 %all-to-all-start = ((bf16[16,128,128]{2,1,0:T(8,128)(2,1)}), bf16[16,128,128]{2,1,0:T(8,128)(2,1)S(1)}, u32[]{:S(2)}, u32[]{:S(2)}) async-start(bf16[16,128,128]{2,1,0:T(8,128)(2,1)} %shard_map.145), calls=%async_computation | async-start | bytes 1048576 | tf_op jit(solution)/shard_map/all_to_all | solution.py:383
  18.4 0.0 copy-done.11
  18.4 0.1 broadcast_in_dim.2
  18.5 0.0 copy-done.9
  18.5 0.1 pad_maximum_fusion.params_ref
  18.6 0.0 copy-done
  18.6 0.0 copy-done.3
  18.6 3.9 %cosine_bitcast_fusion = (f32[64,2048]{1,0:T(8,128)S(1)}, f32[64,2048]{1,0:T(8,128)S(1)}) fusion(f32[32,2048]{1,0:T(8,128)S(1)} %copy-done.3, f32[32,64]{1,0:T(8,128)S(1)} %copy-done), kind=kOutput, calls=%fused_computation | convolution fusion | flops 50331648 | bytes 1318912 | tf_op jit(solution)/shard_map/ej,et->jt/dot_general | solution.py:384
  22.5 0.0 copy-done.1
  22.5 0.0 copy-done.7
  22.5 1.6 %shard_map.146.taps_ref = f32[17,64,256]{2,1,0:T(8,128)S(1)} custom-call(f32[64,2048]{1,0:T(8,128)S(1)} %get-tuple-element.27.hidden_ref, f32[64,128]{1,0:T(8,128)S(1)} %pad_maximum_fusion.params_ref, bf16[2,256,256]{2,1,0:T(8,128)(2,1)S(1)} %copy-done.1, f32[4,24,128]{2,1,0:T(8,128)S(1)} %copy-done.7), custom_call_target="tpu_custom_call" | custom-call | tf_op jit(solution)/shard_map/pallas_call | solution.py:348
  24.1 22.5 %all-to-all-done.got_ref = bf16[16,128,128]{2,1,0:T(8,128)(2,1)S(1)} async-done(((bf16[16,128,128]{2,1,0:T(8,128)(2,1)}), bf16[16,128,128]{2,1,0:T(8,128)(2,1)S(1)}, u32[]{:S(2)}, u32[]{:S(2)}) %all-to-all-start) | async-done | bytes 524320 | tf_op jit(solution)/shard_map/all_to_all | solution.py:383
  46.6 5.9 %shard_map.147 = bf16[32,16,128]{2,1,0:T(8,128)(2,1)} custom-call(bf16[16,128,128]{2,1,0:T(8,128)(2,1)S(1)} %all-to-all-done.got_ref, f32[64,2048]{1,0:T(8,128)S(1)} %get-tuple-element.26.slope_ref, f32[32,2048]{1,0:T(8,128)S(1)} %copy-done.3, f32[64,128]{1,0:T(8,128)S(1)} %pad_maximum_fusion.params_ref, bf16[2,256,256]{2,1,0:T(8,128)(2,1)S(1)} %copy-done.1, ...), custom_call_target="tpu_custom_call" | custom-call | tf_op jit(solution)/shard_map/pallas_call | solution.py:348
  52.6 7.3 %all-to-all-start.1 = ((bf16[32,16,128]{2,1,0:T(8,128)(2,1)}), bf16[32,16,128]{2,1,0:T(8,128)(2,1)S(1)}, u32[]{:S(2)}, u32[]{:S(2)}) async-start(bf16[32,16,128]{2,1,0:T(8,128)(2,1)} %shard_map.147), calls=%async_computation.1 | async-start | bytes 262144 | tf_op jit(solution)/shard_map/all_to_all | solution.py:406
  59.9 6.6 %shard_map.148 = (bf16[16,144,128]{2,1,0:T(8,128)(2,1)S(1)}, f32[64,128]{1,0:T(8,128)S(1)}) custom-call(bf16[16,128,128]{2,1,0:T(8,128)(2,1)S(1)} %all-to-all-done.got_ref, f32[17,64,256]{2,1,0:T(8,128)S(1)} %shard_map.146.taps_ref, f32[64,2048]{1,0:T(8,128)S(1)} %get-tuple-element.27.hidden_ref, f32[64,128]{1,0:T(8,128)S(1)} %pad_maximum_fusion.params_ref, ...), custom_call_target="tpu_custom_call" | custom-call | tf_op jit(solution)/shard_map/pallas_call | solution.py:348
  66.5 0.0 copy-start.2
  66.5 0.8 copy-done.2
  67.3 0.3 all-to-all-done.1.shares_ref
  67.7 0.0 copy-start.8
  67.7 0.7 copy-done.8
  68.3 0.0 copy-start.4
  68.3 0.0 copy-start.5
  68.4 0.0 copy-start.6
  68.4 1.8 %shard_map.149 = bf16[16,144,128]{2,1,0:T(8,128)(2,1)} custom-call(bf16[32,16,128]{2,1,0:T(8,128)(2,1)} %copy-done.8, bf16[16,144,128]{2,1,0:T(8,128)(2,1)} %copy-done.2), custom_call_target="tpu_custom_call", output_to_operand_aliasing={{}: (1, {})} | custom-call | tf_op jit(solution)/shard_map/pallas_call | solution.py:348
  70.2 7.2 %all-to-all-start.2 = ((bf16[16,144,128]{2,1,0:T(8,128)(2,1)}), bf16[16,144,128]{2,1,0:T(8,128)(2,1)S(1)}, u32[]{:S(2)}, u32[]{:S(2)}) async-start(bf16[16,144,128]{2,1,0:T(8,128)(2,1)} %shard_map.149), calls=%async_computation.2 | async-start | bytes 1179648 | tf_op jit(solution)/shard_map/all_to_all | solution.py:430
  77.3 1.9 %collective-permute-start = (f32[64,128]{1,0:T(8,128)S(1)}, f32[64,128]{1,0:T(8,128)S(1)}, u32[]{:S(2)}, u32[]{:S(2)}) collective-permute-start(f32[64,128]{1,0:T(8,128)S(1)} %get-tuple-element.24), channel_id=1, source_target_pairs={{0,128},{128,0},{256,384},{384,256},{1,129},{129,1},{257,385},{385... | collective-permute-start | bytes 98312 | tf_op jit(solution)/shard_map/ppermute | solution.py:361
  79.3 1.2 %collective-permute-done = f32[64,128]{1,0:T(8,128)S(1)} collective-permute-done((f32[64,128]{1,0:T(8,128)S(1)}, f32[64,128]{1,0:T(8,128)S(1)}, u32[]{:S(2)}, u32[]{:S(2)}) %collective-permute-start) | collective-permute-done | bytes 32800 | tf_op jit(solution)/shard_map/ppermute | solution.py:361
  80.4 4.9 %collective-permute-start.1 = (f32[64,128]{1,0:T(8,128)S(1)}, f32[64,128]{1,0:T(8,128)S(1)}, u32[]{:S(2)}, u32[]{:S(2)}) collective-permute-start(f32[64,128]{1,0:T(8,128)S(1)} %add.6), channel_id=1, source_target_pairs={{0,256},{128,384},{256,0},{384,128},{1,257},{129,385},{257,1},{385... | collective-permute-start | bytes 98312 | tf_op jit(solution)/shard_map/ppermute | solution.py:361
  85.3 2.4 %collective-permute-done.1 = f32[64,128]{1,0:T(8,128)S(1)} collective-permute-done((f32[64,128]{1,0:T(8,128)S(1)}, f32[64,128]{1,0:T(8,128)S(1)}, u32[]{:S(2)}, u32[]{:S(2)}) %collective-permute-start.1) | collective-permute-done | bytes 32800 | tf_op jit(solution)/shard_map/ppermute | solution.py:361
  87.8 0.0 copy-start.10
  87.8 0.6 slice_bitcast_fusion
  88.3 20.8 %all-to-all-done.2.got_ref = bf16[16,144,128]{2,1,0:T(8,128)(2,1)S(1)} async-done(((bf16[16,144,128]{2,1,0:T(8,128)(2,1)}), bf16[16,144,128]{2,1,0:T(8,128)(2,1)S(1)}, u32[]{:S(2)}, u32[]{:S(2)}) %all-to-all-start.2) | async-done | bytes 589856 | tf_op jit(solution)/shard_map/all_to_all | solution.py:430
  109.2 0.0 copy-done.4
  109.2 0.0 copy-done.5
  109.2 0.0 copy-done.6
  109.2 1.2 %shard_map.150 = (bf16[1,128,1024]{2,1,0:T(8,128)(2,1)}, bf16[1,128,1024]{2,1,0:T(8,128)(2,1)}, bf16[1,128,1024]{2,1,0:T(8,128)(2,1)}, f32[32,64]{1,0:T(8,128)}) custom-call(bf16[16,144,128]{2,1,0:T(8,128)(2,1)S(1)} %all-to-all-done.2.got_ref, bf16[1,128,1024]{2,1,0:T(8,128)(2,1)S(1)} %copy-done.4, bf16[1,128,1024]{2,1,0:T(8,128)(2,1)S(1)} %copy-done.5, ...), custom_call_target="tpu_custom_call" | custom-call | tf_op jit(solution)/shard_map/pallas_call | solution.py:348
  110.3 0.0 copy-done.10
  (2 shorter events, 0.0 us)
Async XLA Ops:
  0.6 17.9 %copy-start = (f32[32,64]{1,0:T(8,128)S(1)}, f32[32,64]{1,0:T(8,128)}, u32[]{:S(2)}) copy-start(f32[32,64]{1,0:T(8,128)} %param.14) | copy-start | bytes 24580
  0.6 17.9 %copy-start.3 = (f32[32,2048]{1,0:T(8,128)S(1)}, f32[32,2048]{1,0:T(8,128)}, u32[]{:S(2)}) copy-start(f32[32,2048]{1,0:T(8,128)} %constant.8.clone.features_ref) | copy-start | bytes 786436
  0.7 17.8 %copy-start.9 = (f32[64,64]{1,0:T(8,128)S(1)}, f32[64,64]{1,0:T(8,128)}, u32[]{:S(2)}) copy-start(f32[64,64]{1,0:T(8,128)} %param.15) | copy-start | bytes 49156
  0.7 17.7 %copy-start.11 = (f32[64]{0:T(128)S(1)}, f32[64]{0:T(128)}, u32[]{:S(2)}) copy-start(f32[64]{0:T(128)} %param.16) | copy-start | bytes 772
  3.0 19.5 %copy-start.1 = (bf16[2,256,256]{2,1,0:T(8,128)(2,1)S(1)}, bf16[2,256,256]{2,1,0:T(8,128)(2,1)}, u32[]{:S(2)}) copy-start(bf16[2,256,256]{2,1,0:T(8,128)(2,1)} %constant.6.clone.table_ref) | copy-start | bytes 786436
  3.0 19.5 %copy-start.7 = (f32[4,24,128]{2,1,0:T(8,128)S(1)}, f32[4,24,128]{2,1,0:T(8,128)}, u32[]{:S(2)}) copy-start(f32[4,24,128]{2,1,0:T(8,128)} %constant.7.clone.turns_ref) | copy-start | bytes 147460
  3.1 43.6 %all-to-all-start = ((bf16[16,128,128]{2,1,0:T(8,128)(2,1)}), bf16[16,128,128]{2,1,0:T(8,128)(2,1)S(1)}, u32[]{:S(2)}, u32[]{:S(2)}) async-start(bf16[16,128,128]{2,1,0:T(8,128)(2,1)} %shard_map.145), calls=%async_computation | async-start | bytes 1048576 | tf_op jit(solution)/shard_map/all_to_all | solution.py:383
  52.6 15.1 %all-to-all-start.1 = ((bf16[32,16,128]{2,1,0:T(8,128)(2,1)}), bf16[32,16,128]{2,1,0:T(8,128)(2,1)S(1)}, u32[]{:S(2)}, u32[]{:S(2)}) async-start(bf16[32,16,128]{2,1,0:T(8,128)(2,1)} %shard_map.147), calls=%async_computation.1 | async-start | bytes 262144 | tf_op jit(solution)/shard_map/all_to_all | solution.py:406
  66.5 0.8 copy-start.2
  67.7 0.7 copy-start.8
  68.3 40.8 %copy-start.4 = (bf16[1,128,1024]{2,1,0:T(8,128)(2,1)S(1)}, bf16[1,128,1024]{2,1,0:T(8,128)(2,1)}, u32[]{:S(2)}) copy-start(bf16[1,128,1024]{2,1,0:T(8,128)(2,1)} %key_ref.1) | copy-start | bytes 786436
  68.3 40.8 %copy-start.5 = (bf16[1,128,1024]{2,1,0:T(8,128)(2,1)S(1)}, bf16[1,128,1024]{2,1,0:T(8,128)(2,1)}, u32[]{:S(2)}) copy-start(bf16[1,128,1024]{2,1,0:T(8,128)(2,1)} %value_ref.1) | copy-start | bytes 786436
  68.4 40.8 %copy-start.6 = (bf16[1,128,1024]{2,1,0:T(8,128)(2,1)S(1)}, bf16[1,128,1024]{2,1,0:T(8,128)(2,1)}, u32[]{:S(2)}) copy-start(bf16[1,128,1024]{2,1,0:T(8,128)(2,1)} %grad_ref.1) | copy-start | bytes 786436
  70.2 39.0 %all-to-all-start.2 = ((bf16[16,144,128]{2,1,0:T(8,128)(2,1)}), bf16[16,144,128]{2,1,0:T(8,128)(2,1)S(1)}, u32[]{:S(2)}, u32[]{:S(2)}) async-start(bf16[16,144,128]{2,1,0:T(8,128)(2,1)} %shard_map.149), calls=%async_computation.2 | async-start | bytes 1179648 | tf_op jit(solution)/shard_map/all_to_all | solution.py:430
  77.3 3.1 %collective-permute-start = (f32[64,128]{1,0:T(8,128)S(1)}, f32[64,128]{1,0:T(8,128)S(1)}, u32[]{:S(2)}, u32[]{:S(2)}) collective-permute-start(f32[64,128]{1,0:T(8,128)S(1)} %get-tuple-element.24), channel_id=1, source_target_pairs={{0,128},{128,0},{256,384},{384,256},{1,129},{129,1},{257,385},{385... | collective-permute-start | bytes 98312 | tf_op jit(solution)/shard_map/ppermute | solution.py:361
  80.4 7.3 %collective-permute-start.1 = (f32[64,128]{1,0:T(8,128)S(1)}, f32[64,128]{1,0:T(8,128)S(1)}, u32[]{:S(2)}, u32[]{:S(2)}) collective-permute-start(f32[64,128]{1,0:T(8,128)S(1)} %add.6), channel_id=1, source_target_pairs={{0,256},{128,384},{256,0},{384,128},{1,257},{129,385},{257,1},{385... | collective-permute-start | bytes 98312 | tf_op jit(solution)/shard_map/ppermute | solution.py:361
  87.8 22.6 %copy-start.10 = (f32[64,128]{1,0:T(8,128)}, f32[64,128]{1,0:T(8,128)S(1)}, u32[]{:S(2)}) copy-start(f32[64,128]{1,0:T(8,128)S(1)} %add.7) | copy-start | bytes 98308

commit v3 on v2

--- a/solution.py
+++ b/solution.py
@@ -141,11 +141,14 @@
     return high, (values - high.astype(jnp.float32)).astype(jnp.bfloat16)
 
 
-def precise_dot(values, table_ref, side=0):
+def precise_dot(values, table_ref, side=0, brief=False):
     high, low = split(values)
     dims = (((1,), (side,)), ((), ()))
     dot = lambda a, b: lax.dot_general(a, b, dims, preferred_element_type=jnp.float32)
-    return dot(high, table_ref[0]) + (dot(low, table_ref[0]) + dot(high, table_ref[1]))
+    rest = dot(high, table_ref[1])
+    if not brief:
+        rest = dot(low, table_ref[0]) + rest
+    return dot(high, table_ref[0]) + rest
 
 
 def forward_outer(load, rows, turns_ref, turned_ref):
@@ -166,14 +169,13 @@
             turned_ref[k, where, INNER:] = turned_imag
 
 
-def inverse_outer(back_ref, offset, rows, turns_ref, store):
+def inverse_outer(back_ref, rows, turns_ref, store):
     @pl.loop(0, rows // 8)
     def _(step):
         where = pl.ds(pl.multiple_of(step * 8, 8), 8)
-        place = pl.ds(pl.multiple_of(offset + step * 8, 8), 8)
         bins = {}
         for k in range(HALF):
-            real, imag = back_ref[k, place, :INNER], back_ref[k, place, INNER:]
+            real, imag = back_ref[k, where, :INNER], back_ref[k, where, INNER:]
             cos, sin = turns_ref[2, k : k + 1, :], turns_ref[3, k : k + 1, :]
             if k in (0, HALF - 1):
                 bins[k] = (real * cos - imag * sin, None)
@@ -186,28 +188,29 @@
 def pack_kernel(
     query_hbm, key_hbm, value_hbm, grad_hbm, sent_hbm, key_ref, value_ref, grad_ref, query_ref, sent_ref, sems, out_sems
 ):
-    pairs = ((key_hbm, key_ref), (value_hbm, value_ref), (grad_hbm, grad_ref), (query_hbm, query_ref))
-    copies = []
-    for i, (source, target) in enumerate(pairs):
-        for half in range(2):
-            rows = pl.ds(half * (INNER // 2), INNER // 2)
-            copies.append(pltpu.make_async_copy(source.at[0, rows], target.at[rows], sems.at[2 * i + half]))
-            copies[-1].start()
+    sources = (key_hbm, value_hbm, grad_hbm, query_hbm)
+    targets = (key_ref, value_ref, grad_ref, query_ref)
+    copies = {}
+    for part in range(4):
+        lanes = pl.ds(4 * GROUP * part, 4 * GROUP)
+        for i in range(4):
+            source, target = sources[i].at[0, :, lanes], targets[i].at[:, lanes]
+            copies[part, i] = pltpu.make_async_copy(source, target, sems.at[4 * part + i])
+            copies[part, i].start()
     outs = []
-    for part, (first, second) in enumerate(((key_ref, value_ref), (grad_ref, query_ref))):
-        place = part * GROUP
-        for copy in copies[4 * part : 4 * part + 4]:
-            copy.wait()
-        for pair in range(BLOCKS // 2):
+    for part in range(4):
+        for i in range(4):
+            copies[part, i].wait()
+        for pair in (2 * part, 2 * part + 1):
             lanes = slice(2 * GROUP * pair, 2 * GROUP * (pair + 1))
-            both = first[:, lanes].astype(jnp.float32) * second[:, lanes].astype(jnp.float32)
-            both = both.T.astype(jnp.bfloat16)
-            sent_ref[2 * pair, place : place + GROUP] = both[:GROUP]
-            sent_ref[2 * pair + 1, place : place + GROUP] = both[GROUP:]
-            if part == 1 and pair % 2 == 1:
-                where = pl.ds(2 * (pair - 1), 4)
-                outs.append(pltpu.make_async_copy(sent_ref.at[where], sent_hbm.at[where], out_sems.at[pair // 2]))
-                outs[-1].start()
+            for place, first, second in ((0, key_ref, value_ref), (GROUP, grad_ref, query_ref)):
+                both = first[:, lanes].astype(jnp.float32) * second[:, lanes].astype(jnp.float32)
+                both = both.T.astype(jnp.bfloat16)
+                sent_ref[2 * pair, place : place + GROUP] = both[:GROUP]
+                sent_ref[2 * pair + 1, place : place + GROUP] = both[GROUP:]
+        where = pl.ds(4 * part, 4)
+        outs.append(pltpu.make_async_copy(sent_ref.at[where], sent_hbm.at[where], out_sems.at[part]))
+        outs[-1].start()
     for copy in outs:
         copy.wait()
 
@@ -238,10 +241,10 @@
     return dot(a_high, b_high) + (dot(a_low, b_high) + dot(a_high, b_low))
 
 
-def spectra(turned_ref, table_ref, first, last):
+def spectra(turned_ref, table_ref, first, last, brief=False):
     count = last - first
     turned = turned_ref[first:last].reshape(count * 2 * GROUP, 2 * INNER)
-    spec = precise_dot(turned, table_ref).reshape(count, 2 * GROUP, 2 * INNER)
+    spec = precise_dot(turned, table_ref, brief=brief).reshape(count, 2 * GROUP, 2 * INNER)
     in_real, in_imag = spec[:, :GROUP, :INNER], spec[:, :GROUP, INNER:]
     up_real, up_imag = spec[:, GROUP:, :INNER], spec[:, GROUP:, INNER:]
     corr = pair(in_real * up_real + in_imag * up_imag, in_real * up_imag - in_imag * up_real)
@@ -257,11 +260,17 @@
     forward_outer(lambda n, where: wide_ref[n, where, :], 2 * GROUP, turns_ref, turned_ref)
 
 
-def weighted_corr(back_ref, offset, params_ref, turns_ref, corr_time_ref):
+def weighted_corr(got_ref, params_ref, table_ref, turns_ref, wide_ref, turned_ref, back_ref, corr_time_ref, brief):
+    forward_both(got_ref, wide_ref, turns_ref, turned_ref)
+    for first, last in PARTS:
+        corr = spectra(turned_ref, table_ref, first, last, brief)[4]
+        back = precise_dot(corr.reshape((last - first) * GROUP, 2 * INNER), table_ref, 1, brief)
+        back_ref[first:last] = back.reshape(last - first, GROUP, 2 * INNER)
+
     def store(n, where, value):
         corr_time_ref[where, n * INNER : (n + 1) * INNER] = value * np.float32(1.0 / math.sqrt(4 * LENGTH))
 
-    inverse_outer(back_ref, offset, GROUP, turns_ref, store)
+    inverse_outer(back_ref, GROUP, turns_ref, store)
     return corr_time_ref[...] * decay_window(params_ref)
 
 
@@ -273,39 +282,41 @@
 def embed_kernel(
     got_ref, slope_ref, features_ref, params_ref, table_ref, turns_ref, share_ref, wide_ref, turned_ref, back_ref, corr_time_ref
 ):
-    forward_both(got_ref, wide_ref, turns_ref, turned_ref)
-    for first, last in PARTS:
-        corr = spectra(turned_ref, table_ref, first, last)[4]
-        back = precise_dot(corr.reshape((last - first) * GROUP, 2 * INNER), table_ref, 1)
-        back_ref[first:last] = back.reshape(last - first, GROUP, 2 * INNER)
-    weighted = weighted_corr(back_ref, 0, params_ref, turns_ref, corr_time_ref)
+    weighted = weighted_corr(
+        got_ref, params_ref, table_ref, turns_ref, wide_ref, turned_ref, back_ref, corr_time_ref, True
+    )
     hidden_grad = precise(params_ref[:, :GROUP], weighted, ((1,), (0,))) * slope_ref[...]
     embed = precise(features_ref[...], hidden_grad, ALONG) * TIME_SCALE
     embed = jnp.concatenate([embed[:16], embed[16:]], axis=1).astype(jnp.bfloat16)
     share_ref[...] = jnp.broadcast_to(embed[None], share_ref.shape)
 
 
-def main_kernel(
-    got_ref, taps_ref, hidden_ref, params_ref, table_ref, turns_ref, out_ref, grads_ref, wide_ref, turned_ref, back_ref, corr_time_ref
-):
+def conv_kernel(got_ref, taps_ref, table_ref, turns_ref, out_ref, wide_ref, turned_ref, back_ref):
     forward_both(got_ref, wide_ref, turns_ref, turned_ref)
     for first, last in PARTS:
-        in_real, in_imag, up_real, up_imag, corr = spectra(turned_ref, table_ref, first, last)
+        in_real, in_imag, up_real, up_imag, _ = spectra(turned_ref, table_ref, first, last)
         tap_real, tap_imag = taps_ref[first:last, :, :INNER], taps_ref[first:last, :, INNER:]
         conv = pair(tap_real * in_real - tap_imag * in_imag, tap_real * in_imag + tap_imag * in_real)
         grad = pair(tap_real * up_real + tap_imag * up_imag, tap_real * up_imag - tap_imag * up_real)
-        joined = jnp.concatenate([conv, grad, corr], axis=1)
-        back = precise_dot(joined.reshape((last - first) * 3 * GROUP, 2 * INNER), table_ref, 1)
-        back_ref[first:last] = back.reshape(last - first, 3 * GROUP, 2 * INNER)
+        joined = jnp.concatenate([conv, grad], axis=1)
+        back = precise_dot(joined.reshape((last - first) * 2 * GROUP, 2 * INNER), table_ref, 1)
+        back_ref[first:last] = back.reshape(last - first, 2 * GROUP, 2 * INNER)
 
     def store(n, where, value):
         wide_ref[n, where, :] = value
 
-    inverse_outer(back_ref, 0, 2 * GROUP, turns_ref, store)
+    inverse_outer(back_ref, 2 * GROUP, turns_ref, store)
     for n in range(BLOCKS):
         out_ref[n, : 2 * GROUP] = wide_ref[n].astype(jnp.bfloat16)
         out_ref[n, 2 * GROUP :] = jnp.zeros((16, INNER), jnp.bfloat16)
-    weighted = weighted_corr(back_ref, 2 * GROUP, params_ref, turns_ref, corr_time_ref)
+
+
+def grads_kernel(
+    got_ref, hidden_ref, params_ref, table_ref, turns_ref, grads_ref, wide_ref, turned_ref, back_ref, corr_time_ref
+):
+    weighted = weighted_corr(
+        got_ref, params_ref, table_ref, turns_ref, wide_ref, turned_ref, back_ref, corr_time_ref, False
+    )
     grads_ref[:, :GROUP] = precise(hidden_ref[...], weighted, ALONG) * TIME_SCALE
     slopes = weighted * precise(params_ref[:, :GROUP], hidden_ref[...], ((0,), (0,)))
     inner = lax.broadcasted_iota(jnp.int32, (1, INNER), 1)
@@ -375,7 +386,7 @@
         [(moved, bf16)],
         (query_input, key_input, value_input, grad_output),
         [pltpu.VMEM(piece, bf16)] * 4
-        + [pltpu.VMEM(moved, bf16), pltpu.SemaphoreType.DMA((8,)), pltpu.SemaphoreType.DMA((4,))],
+        + [pltpu.VMEM(moved, bf16), pltpu.SemaphoreType.DMA((16,)), pltpu.SemaphoreType.DMA((4,))],
         in_specs=[HBM] * 4,
         out_specs=[HBM],
         megabytes=58,
@@ -396,25 +407,21 @@
     plane = ("dp", "chan")
     both = (HALF, 2 * GROUP, 2 * INNER)
     got, taps_spec = lax.optimization_barrier((got, taps_spec))
+    corr_scratch = [pltpu.VMEM(shape, f32) for shape in (moved, both, spectrum, flat)]
     (shares,) = call(
         embed_kernel,
         [((lax.axis_size(plane), 16, INNER), bf16)],
         (got, slope, features, params, forward, turns),
-        [pltpu.VMEM(moved, f32), pltpu.VMEM(both, f32), pltpu.VMEM(spectrum, f32), pltpu.VMEM(flat, f32)],
+        corr_scratch,
         megabytes=24,
     )
     shares = lax.all_to_all(shares, plane, split_axis=0, concat_axis=0, tiled=True)
-    result, grads = call(
-        main_kernel,
-        [(loaded, bf16), ((GROUP, 2 * GROUP), f32)],
-        (got, taps_spec, hidden, params, forward, turns),
-        [
-            pltpu.VMEM(moved, f32),
-            pltpu.VMEM(both, f32),
-            pltpu.VMEM((HALF, 3 * GROUP, 2 * INNER), f32),
-            pltpu.VMEM(flat, f32),
-        ],
-        megabytes=28,
+    (result,) = call(
+        conv_kernel,
+        [(loaded, bf16)],
+        (got, taps_spec, forward, turns),
+        [pltpu.VMEM(moved, f32), pltpu.VMEM(both, f32), pltpu.VMEM(both, f32)],
+        megabytes=24,
     )
     (result,) = call(
         insert_kernel,
@@ -424,10 +431,17 @@
         in_specs=[VMEM, HBM],
         out_specs=[HBM],
         aliases=((1, 0),),
-        megabytes=58,
-    )
-    result, grads = lax.optimization_barrier((result, grads))
+        megabytes=4,
+    )
+    result, got = lax.optimization_barrier((result, got))
     back = lax.all_to_all(result, "seq", split_axis=0, concat_axis=0, tiled=True)
+    (grads,) = call(
+        grads_kernel,
+        [((GROUP, 2 * GROUP), f32)],
+        (got, hidden, params, forward, turns),
+        corr_scratch,
+        megabytes=24,
+    )
     grads = swapped_sum(swapped_sum(grads, "dp", 1), "dp", 2)
     d_query, d_key, d_value, grad_embed = call(
         apply_kernel,

time: 111 us -> 108 us (0.973)
  starting transfers between devices: 36.6 us -> 34.8 us
  Pallas kernels: 19.4 us -> 21.1 us
  local copies, waits for them, and re-layouts: 2.2 us -> 0.72 us
    all_to_all x1, waiting for transfers between devices: 20.8 us -> 15.6 us  [per_device(): lax.all_to_all(result, 'seq', split_axis=0, concat_axis=0, tiled=True)]
    all_to_all x1, waiting for transfers between devices: 0.34 us -> 2.82 us  [per_device(): lax.all_to_all(shares, plane, split_axis=0, concat_axis=0, tiled=True)]
    ppermute x2, waiting for transfers between devices: 3.61 us -> 5.56 us  [swapped_sum(): lax.ppermute(value, axis, [(i, i ^ step) for i in range(size)])]
    ppermute x2, starting transfers between devices: 6.77 us -> 4.84 us  [swapped_sum(): lax.ppermute(value, axis, [(i, i ^ step) for i in range(size)])]
    pallas_call x6 -> x7, Pallas kernels: 19.4 us -> 21.1 us  [call(): pl.pallas_call(kernel, out_shape=[jax.ShapeDtypeStruct(shape, dtype) for...]
    unnamed x24 -> x20, local copies, waits for them, and re-layouts: 1.55 us -> 0.06 us
  transfers between devices with their start and end apart: 5 -> 5, of which waited for: 5 -> 5; matrix products, arithmetic and copies ran while one was open for 4% -> 4% of each run, Pallas kernels for 7% -> 11%
where the time goes in v3:
time: 108 us
  waiting for transfers between devices  46.5 us (43%)
  starting transfers between devices  34.8 us (32%)
  Pallas kernels  21.1 us (20%)
  matrix products  3.92 us (4%)
    all_to_all x1, waiting for transfers between devices, per_device(): got = lax.all_to_all(sent, 'seq', split_axis=0, concat_axis=0, tiled=True)  22.5 us
    pallas_call x7, Pallas kernels, call(): pl.pallas_call(kernel, out_shape=[jax.ShapeDtypeStruct(shape, dtype) for...  21.1 us
    all_to_all x1, waiting for transfers between devices, per_device(): lax.all_to_all(result, 'seq', split_axis=0, concat_axis=0, tiled=True)  15.6 us
    all_to_all x1, starting transfers between devices, per_device(): got = lax.all_to_all(sent, 'seq', split_axis=0, concat_axis=0, tiled=True)  15.4 us
    all_to_all x1, starting transfers between devices, per_device(): lax.all_to_all(shares, plane, split_axis=0, concat_axis=0, tiled=True)  7.32 us
    all_to_all x1, starting transfers between devices, per_device(): lax.all_to_all(result, 'seq', split_axis=0, concat_axis=0, tiled=True)  7.31 us
    ppermute x2, waiting for transfers between devices, swapped_sum(): lax.ppermute(value, axis, [(i, i ^ step) for i in range(size)])  5.56 us
    ppermute x2, starting transfers between devices, swapped_sum(): lax.ppermute(value, axis, [(i, i ^ step) for i in range(size)])  4.84 us
  transfers between devices with their start and end apart: 5, of which 5 were waited for; matrix products, arithmetic and copies ran while one was open for 4% of the time, Pallas kernels for 11%

profile of v3, /device:TPU:32, one launch (start us, length us, event | category | flops | bytes accessed | tf_op | source)
XLA Modules:
  0.0 107.9 jit_solution(13377553104950390918)
XLA Ops:
  0.6 0.0 copy-start
  0.6 0.0 copy-start.2
  0.7 0.0 copy-start.7
  0.7 0.0 copy-start.9
  0.7 2.3 %shard_map.145 = bf16[16,128,128]{2,1,0:T(8,128)(2,1)} custom-call(bf16[1,128,1024]{2,1,0:T(8,128)(2,1)} %query_hbm.1, bf16[1,128,1024]{2,1,0:T(8,128)(2,1)} %key_ref.1, bf16[1,128,1024]{2,1,0:T(8,128)(2,1)} %value_ref.1, bf16[1,128,1024]{2,1,0:T(8,128)(2,1)} %grad_ref.1), custom_call_target="tpu_custom_call" | custom-call | tf_op jit(solution)/shard_map/pallas_call | solution.py:359
  3.0 0.0 copy-start.1
  3.0 0.0 copy-start.6
  3.0 15.4 %all-to-all-start = ((bf16[16,128,128]{2,1,0:T(8,128)(2,1)}), bf16[16,128,128]{2,1,0:T(8,128)(2,1)S(1)}, u32[]{:S(2)}, u32[]{:S(2)}) async-start(bf16[16,128,128]{2,1,0:T(8,128)(2,1)} %shard_map.145), calls=%async_computation | async-start | bytes 1048576 | tf_op jit(solution)/shard_map/all_to_all | solution.py:394
  18.3 0.0 copy-done.9
  18.3 0.1 broadcast_in_dim.2
  18.4 0.0 copy-done.7
  18.4 0.1 pad_maximum_fusion.params_ref
  18.5 0.0 copy-done
  18.5 0.0 copy-done.2
  18.5 3.9 %cosine_bitcast_fusion = (f32[64,2048]{1,0:T(8,128)S(1)}, f32[64,2048]{1,0:T(8,128)S(1)}) fusion(f32[32,2048]{1,0:T(8,128)S(1)} %copy-done.2, f32[32,64]{1,0:T(8,128)S(1)} %copy-done), kind=kOutput, calls=%fused_computation | convolution fusion | flops 50331648 | bytes 1318912 | tf_op jit(solution)/shard_map/ej,et->jt/dot_general | solution.py:395
  22.4 0.0 copy-done.1
  22.5 0.0 copy-done.6
  22.5 1.6 %shard_map.146.taps_ref = f32[17,64,256]{2,1,0:T(8,128)S(1)} custom-call(f32[64,2048]{1,0:T(8,128)S(1)} %get-tuple-element.23.hidden_ref, f32[64,128]{1,0:T(8,128)S(1)} %pad_maximum_fusion.params_ref, bf16[2,256,256]{2,1,0:T(8,128)(2,1)S(1)} %copy-done.1, f32[4,24,128]{2,1,0:T(8,128)S(1)} %copy-done.6), custom_call_target="tpu_custom_call" | custom-call | tf_op jit(solution)/shard_map/pallas_call | solution.py:359
  24.1 22.5 %all-to-all-done.got_ref = bf16[16,128,128]{2,1,0:T(8,128)(2,1)S(1)} async-done(((bf16[16,128,128]{2,1,0:T(8,128)(2,1)}), bf16[16,128,128]{2,1,0:T(8,128)(2,1)S(1)}, u32[]{:S(2)}, u32[]{:S(2)}) %all-to-all-start) | async-done | bytes 524320 | tf_op jit(solution)/shard_map/all_to_all | solution.py:394
  46.6 5.0 %shard_map.147 = bf16[32,16,128]{2,1,0:T(8,128)(2,1)} custom-call(bf16[16,128,128]{2,1,0:T(8,128)(2,1)S(1)} %all-to-all-done.got_ref, f32[64,2048]{1,0:T(8,128)S(1)} %get-tuple-element.22.slope_ref, f32[32,2048]{1,0:T(8,128)S(1)} %copy-done.2, f32[64,128]{1,0:T(8,128)S(1)} %pad_maximum_fusion.params_ref, bf16[2,256,256]{2,1,0:T(8,128)(2,1)S(1)} %copy-done.1, ...), custom_call_target="tpu_custom_call" | custom-call | tf_op jit(solution)/shard_map/pallas_call | solution.py:359
  51.6 7.3 %all-to-all-start.1 = ((bf16[32,16,128]{2,1,0:T(8,128)(2,1)}), bf16[32,16,128]{2,1,0:T(8,128)(2,1)S(1)}, u32[]{:S(2)}, u32[]{:S(2)}) async-start(bf16[32,16,128]{2,1,0:T(8,128)(2,1)} %shard_map.147), calls=%async_computation.1 | async-start | bytes 262144 | tf_op jit(solution)/shard_map/all_to_all | solution.py:418
  58.9 5.0 %shard_map.148._ = bf16[16,144,128]{2,1,0:T(8,128)(2,1)} custom-call(bf16[16,128,128]{2,1,0:T(8,128)(2,1)S(1)} %all-to-all-done.got_ref, f32[17,64,256]{2,1,0:T(8,128)S(1)} %shard_map.146.taps_ref, bf16[2,256,256]{2,1,0:T(8,128)(2,1)S(1)} %copy-done.1, f32[4,24,128]{2,1,0:T(8,128)S(1)} %copy-done.6), custom_call_target="tpu_custom_call" | custom-call | tf_op jit(solution)/shard_map/pallas_call | solution.py:359
  63.9 2.8 %all-to-all-done.1.shares_ref = bf16[32,16,128]{2,1,0:T(8,128)(2,1)S(1)} async-done(((bf16[32,16,128]{2,1,0:T(8,128)(2,1)}), bf16[32,16,128]{2,1,0:T(8,128)(2,1)S(1)}, u32[]{:S(2)}, u32[]{:S(2)}) %all-to-all-start.1) | async-done | bytes 131104 | tf_op jit(solution)/shard_map/all_to_all | solution.py:418
  66.7 0.8 shard_map.149
  67.6 0.0 copy-start.3
  67.6 0.0 copy-start.4
  67.6 0.0 copy-start.5
  67.6 7.3 %all-to-all-start.2 = ((bf16[16,144,128]{2,1,0:T(8,128)(2,1)}), bf16[16,144,128]{2,1,0:T(8,128)(2,1)S(1)}, u32[]{:S(2)}, u32[]{:S(2)}) async-start(bf16[16,144,128]{2,1,0:T(8,128)(2,1)} %shard_map.149), calls=%async_computation.2 | async-start | bytes 1179648 | tf_op jit(solution)/shard_map/all_to_all | solution.py:437
  74.9 5.2 %shard_map.151 = f32[64,128]{1,0:T(8,128)S(1)} custom-call(bf16[16,128,128]{2,1,0:T(8,128)(2,1)S(1)} %all-to-all-done.got_ref, f32[64,2048]{1,0:T(8,128)S(1)} %get-tuple-element.23.hidden_ref, f32[64,128]{1,0:T(8,128)S(1)} %pad_maximum_fusion.params_ref, bf16[2,256,256]{2,1,0:T(8,128)(2,1)S(1)} %copy-done.1, f32[4,24,128]{2,1,0:T(8,128)S(1)} %copy-done.6), custom_call_target="tpu_custom_call" | custom-call | tf_op jit(solution)/shard_map/pallas_call | solution.py:359
  80.1 1.9 %collective-permute-start = (f32[64,128]{1,0:T(8,128)S(1)}, f32[64,128]{1,0:T(8,128)S(1)}, u32[]{:S(2)}, u32[]{:S(2)}) collective-permute-start(f32[64,128]{1,0:T(8,128)S(1)} %shard_map.151), channel_id=1, source_target_pairs={{0,128},{128,0},{256,384},{384,256},{1,129},{129,1},{257,385},{385... | collective-permute-start | bytes 98312 | tf_op jit(solution)/shard_map/ppermute | solution.py:372
  82.0 1.2 %collective-permute-done = f32[64,128]{1,0:T(8,128)S(1)} collective-permute-done((f32[64,128]{1,0:T(8,128)S(1)}, f32[64,128]{1,0:T(8,128)S(1)}, u32[]{:S(2)}, u32[]{:S(2)}) %collective-permute-start) | collective-permute-done | bytes 32800 | tf_op jit(solution)/shard_map/ppermute | solution.py:372
  83.2 2.9 %collective-permute-start.1 = (f32[64,128]{1,0:T(8,128)S(1)}, f32[64,128]{1,0:T(8,128)S(1)}, u32[]{:S(2)}, u32[]{:S(2)}) collective-permute-start(f32[64,128]{1,0:T(8,128)S(1)} %add.6), channel_id=1, source_target_pairs={{0,256},{128,384},{256,0},{384,128},{1,257},{129,385},{257,1},{385... | collective-permute-start | bytes 98312 | tf_op jit(solution)/shard_map/ppermute | solution.py:372
  86.1 4.4 %collective-permute-done.1 = f32[64,128]{1,0:T(8,128)S(1)} collective-permute-done((f32[64,128]{1,0:T(8,128)S(1)}, f32[64,128]{1,0:T(8,128)S(1)}, u32[]{:S(2)}, u32[]{:S(2)}) %collective-permute-start.1) | collective-permute-done | bytes 32800 | tf_op jit(solution)/shard_map/ppermute | solution.py:372
  90.5 0.0 copy-start.8
  90.5 0.6 slice_bitcast_fusion
  91.1 15.6 %all-to-all-done.2.got_ref = bf16[16,144,128]{2,1,0:T(8,128)(2,1)S(1)} async-done(((bf16[16,144,128]{2,1,0:T(8,128)(2,1)}), bf16[16,144,128]{2,1,0:T(8,128)(2,1)S(1)}, u32[]{:S(2)}, u32[]{:S(2)}) %all-to-all-start.2) | async-done | bytes 589856 | tf_op jit(solution)/shard_map/all_to_all | solution.py:437
  106.7 0.0 copy-done.3
  106.7 0.0 copy-done.4
  106.7 0.0 copy-done.5
  106.7 1.2 %shard_map.150 = (bf16[1,128,1024]{2,1,0:T(8,128)(2,1)}, bf16[1,128,1024]{2,1,0:T(8,128)(2,1)}, bf16[1,128,1024]{2,1,0:T(8,128)(2,1)}, f32[32,64]{1,0:T(8,128)}) custom-call(bf16[16,144,128]{2,1,0:T(8,128)(2,1)S(1)} %all-to-all-done.2.got_ref, bf16[1,128,1024]{2,1,0:T(8,128)(2,1)S(1)} %copy-done.3, bf16[1,128,1024]{2,1,0:T(8,128)(2,1)S(1)} %copy-done.4, ...), custom_call_target="tpu_custom_call" | custom-call | tf_op jit(solution)/shard_map/pallas_call | solution.py:359
  107.9 0.0 copy-done.8
  (2 shorter events, 0.0 us)
Async XLA Ops:
  0.6 17.9 %copy-start = (f32[32,64]{1,0:T(8,128)S(1)}, f32[32,64]{1,0:T(8,128)}, u32[]{:S(2)}) copy-start(f32[32,64]{1,0:T(8,128)} %param.14) | copy-start | bytes 24580
  0.6 17.9 %copy-start.2 = (f32[32,2048]{1,0:T(8,128)S(1)}, f32[32,2048]{1,0:T(8,128)}, u32[]{:S(2)}) copy-start(f32[32,2048]{1,0:T(8,128)} %constant.8.clone.features_ref) | copy-start | bytes 786436
  0.7 17.8 %copy-start.7 = (f32[64,64]{1,0:T(8,128)S(1)}, f32[64,64]{1,0:T(8,128)}, u32[]{:S(2)}) copy-start(f32[64,64]{1,0:T(8,128)} %param.15) | copy-start | bytes 49156
  0.7 17.7 %copy-start.9 = (f32[64]{0:T(128)S(1)}, f32[64]{0:T(128)}, u32[]{:S(2)}) copy-start(f32[64]{0:T(128)} %param.16) | copy-start | bytes 772
  3.0 19.5 %copy-start.1 = (bf16[2,256,256]{2,1,0:T(8,128)(2,1)S(1)}, bf16[2,256,256]{2,1,0:T(8,128)(2,1)}, u32[]{:S(2)}) copy-start(bf16[2,256,256]{2,1,0:T(8,128)(2,1)} %constant.6.clone.table_ref) | copy-start | bytes 786436
  3.0 19.5 %copy-start.6 = (f32[4,24,128]{2,1,0:T(8,128)S(1)}, f32[4,24,128]{2,1,0:T(8,128)}, u32[]{:S(2)}) copy-start(f32[4,24,128]{2,1,0:T(8,128)} %constant.7.clone.turns_ref) | copy-start | bytes 147460
  3.0 43.6 %all-to-all-start = ((bf16[16,128,128]{2,1,0:T(8,128)(2,1)}), bf16[16,128,128]{2,1,0:T(8,128)(2,1)S(1)}, u32[]{:S(2)}, u32[]{:S(2)}) async-start(bf16[16,128,128]{2,1,0:T(8,128)(2,1)} %shard_map.145), calls=%async_computation | async-start | bytes 1048576 | tf_op jit(solution)/shard_map/all_to_all | solution.py:394
  51.6 15.1 %all-to-all-start.1 = ((bf16[32,16,128]{2,1,0:T(8,128)(2,1)}), bf16[32,16,128]{2,1,0:T(8,128)(2,1)S(1)}, u32[]{:S(2)}, u32[]{:S(2)}) async-start(bf16[32,16,128]{2,1,0:T(8,128)(2,1)} %shard_map.147), calls=%async_computation.1 | async-start | bytes 262144 | tf_op jit(solution)/shard_map/all_to_all | solution.py:418
  67.6 39.2 %copy-start.3 = (bf16[1,128,1024]{2,1,0:T(8,128)(2,1)S(1)}, bf16[1,128,1024]{2,1,0:T(8,128)(2,1)}, u32[]{:S(2)}) copy-start(bf16[1,128,1024]{2,1,0:T(8,128)(2,1)} %key_ref.1) | copy-start | bytes 786436
  67.6 39.1 %copy-start.4 = (bf16[1,128,1024]{2,1,0:T(8,128)(2,1)S(1)}, bf16[1,128,1024]{2,1,0:T(8,128)(2,1)}, u32[]{:S(2)}) copy-start(bf16[1,128,1024]{2,1,0:T(8,128)(2,1)} %value_ref.1) | copy-start | bytes 786436
  67.6 39.1 %copy-start.5 = (bf16[1,128,1024]{2,1,0:T(8,128)(2,1)S(1)}, bf16[1,128,1024]{2,1,0:T(8,128)(2,1)}, u32[]{:S(2)}) copy-start(bf16[1,128,1024]{2,1,0:T(8,128)(2,1)} %grad_ref.1) | copy-start | bytes 786436
  67.6 39.1 %all-to-all-start.2 = ((bf16[16,144,128]{2,1,0:T(8,128)(2,1)}), bf16[16,144,128]{2,1,0:T(8,128)(2,1)S(1)}, u32[]{:S(2)}, u32[]{:S(2)}) async-start(bf16[16,144,128]{2,1,0:T(8,128)(2,1)} %shard_map.149), calls=%async_computation.2 | async-start | bytes 1179648 | tf_op jit(solution)/shard_map/all_to_all | solution.py:437
  80.1 3.1 %collective-permute-start = (f32[64,128]{1,0:T(8,128)S(1)}, f32[64,128]{1,0:T(8,128)S(1)}, u32[]{:S(2)}, u32[]{:S(2)}) collective-permute-start(f32[64,128]{1,0:T(8,128)S(1)} %shard_map.151), channel_id=1, source_target_pairs={{0,128},{128,0},{256,384},{384,256},{1,129},{129,1},{257,385},{385... | collective-permute-start | bytes 98312 | tf_op jit(solution)/shard_map/ppermute | solution.py:372
  83.2 7.3 %collective-permute-start.1 = (f32[64,128]{1,0:T(8,128)S(1)}, f32[64,128]{1,0:T(8,128)S(1)}, u32[]{:S(2)}, u32[]{:S(2)}) collective-permute-start(f32[64,128]{1,0:T(8,128)S(1)} %add.6), channel_id=1, source_target_pairs={{0,256},{128,384},{256,0},{384,128},{1,257},{129,385},{257,1},{385... | collective-permute-start | bytes 98312 | tf_op jit(solution)/shard_map/ppermute | solution.py:372
  90.5 17.4 %copy-start.8 = (f32[64,128]{1,0:T(8,128)}, f32[64,128]{1,0:T(8,128)S(1)}, u32[]{:S(2)}) copy-start(f32[64,128]{1,0:T(8,128)S(1)} %add.7) | copy-start | bytes 98308

commit v4 on v3

--- a/solution.py
+++ b/solution.py
@@ -152,7 +152,7 @@
 
 
 def forward_outer(load, rows, turns_ref, turned_ref):
-    @pl.loop(0, rows // 8)
+    @pl.loop(0, rows // 8, unroll=2)
     def _(step):
         where = pl.ds(pl.multiple_of(step * 8, 8), 8)
         bins = outer_bins([load(n, where) for n in range(BLOCKS)])
@@ -170,7 +170,7 @@
 
 
 def inverse_outer(back_ref, rows, turns_ref, store):
-    @pl.loop(0, rows // 8)
+    @pl.loop(0, rows // 8, unroll=2)
     def _(step):
         where = pl.ds(pl.multiple_of(step * 8, 8), 8)
         bins = {}
@@ -285,8 +285,19 @@
     weighted = weighted_corr(
         got_ref, params_ref, table_ref, turns_ref, wide_ref, turned_ref, back_ref, corr_time_ref, True
     )
-    hidden_grad = precise(params_ref[:, :GROUP], weighted, ((1,), (0,))) * slope_ref[...]
-    embed = precise(features_ref[...], hidden_grad, ALONG) * TIME_SCALE
+    (filter_high, filter_low), (high, low) = split(params_ref[:, :GROUP]), split(weighted)
+    hidden_grad = slope_ref[...] * jnp.dot(
+        jnp.concatenate([filter_high, filter_low, filter_high], axis=1),
+        jnp.concatenate([high, high, low], axis=0),
+        preferred_element_type=jnp.float32,
+    )
+    crossed = lax.dot_general(
+        jnp.concatenate(split(features_ref[...]), axis=0),
+        jnp.concatenate(split(hidden_grad), axis=0),
+        (ALONG, ((), ())),
+        preferred_element_type=jnp.float32,
+    )
+    embed = (crossed[:32, :GROUP] + (crossed[32:, :GROUP] + crossed[:32, GROUP:])) * TIME_SCALE
     embed = jnp.concatenate([embed[:16], embed[16:]], axis=1).astype(jnp.bfloat16)
     share_ref[...] = jnp.broadcast_to(embed[None], share_ref.shape)
 

time: 108 us -> 108 us (level)
  no operation moved by 1% of the time
where the time goes in v4:
time: 108 us
  waiting for transfers between devices  46.7 us (43%)
  starting transfers between devices  34.8 us (32%)
  Pallas kernels  20.5 us (19%)
  matrix products  3.92 us (4%)
    all_to_all x1, waiting for transfers between devices, per_device(): got = lax.all_to_all(sent, 'seq', split_axis=0, concat_axis=0, tiled=True)  22.5 us
    pallas_call x7, Pallas kernels, call(): pl.pallas_call(kernel, out_shape=[jax.ShapeDtypeStruct(shape, dtype) for...  20.5 us
    all_to_all x1, waiting for transfers between devices, per_device(): lax.all_to_all(result, 'seq', split_axis=0, concat_axis=0, tiled=True)  15.7 us
    all_to_all x1, starting transfers between devices, per_device(): got = lax.all_to_all(sent, 'seq', split_axis=0, concat_axis=0, tiled=True)  15.4 us
    all_to_all x1, starting transfers between devices, per_device(): lax.all_to_all(shares, plane, split_axis=0, concat_axis=0, tiled=True)  7.32 us
    all_to_all x1, starting transfers between devices, per_device(): lax.all_to_all(result, 'seq', split_axis=0, concat_axis=0, tiled=True)  7.3 us
    ppermute x2, waiting for transfers between devices, swapped_sum(): lax.ppermute(value, axis, [(i, i ^ step) for i in range(size)])  5.56 us
    ppermute x2, starting transfers between devices, swapped_sum(): lax.ppermute(value, axis, [(i, i ^ step) for i in range(size)])  4.84 us
  transfers between devices with their start and end apart: 5, of which 5 were waited for; matrix products, arithmetic and copies ran while one was open for 4% of the time, Pallas kernels for 11%

profile of v4, /device:TPU:32, one launch (start us, length us, event | category | flops | bytes accessed | tf_op | source)
XLA Modules:
  0.0 107.6 jit_solution(16521052595725729320)
XLA Ops:
  0.6 0.0 copy-start
  0.6 0.0 copy-start.2
  0.7 0.0 copy-start.7
  0.7 0.0 copy-start.9
  0.7 2.3 %shard_map.145 = bf16[16,128,128]{2,1,0:T(8,128)(2,1)} custom-call(bf16[1,128,1024]{2,1,0:T(8,128)(2,1)} %query_hbm.1, bf16[1,128,1024]{2,1,0:T(8,128)(2,1)} %key_ref.1, bf16[1,128,1024]{2,1,0:T(8,128)(2,1)} %value_ref.1, bf16[1,128,1024]{2,1,0:T(8,128)(2,1)} %grad_ref.1), custom_call_target="tpu_custom_call" | custom-call | tf_op jit(solution)/shard_map/pallas_call | solution.py:370
  3.0 0.0 copy-start.1
  3.0 0.0 copy-start.6
  3.0 15.4 %all-to-all-start = ((bf16[16,128,128]{2,1,0:T(8,128)(2,1)}), bf16[16,128,128]{2,1,0:T(8,128)(2,1)S(1)}, u32[]{:S(2)}, u32[]{:S(2)}) async-start(bf16[16,128,128]{2,1,0:T(8,128)(2,1)} %shard_map.145), calls=%async_computation | async-start | bytes 1048576 | tf_op jit(solution)/shard_map/all_to_all | solution.py:405
  18.3 0.0 copy-done.9
  18.3 0.1 broadcast_in_dim.2
  18.4 0.0 copy-done.7
  18.4 0.1 pad_maximum_fusion.params_ref
  18.5 0.0 copy-done
  18.5 0.0 copy-done.2
  18.5 3.9 %cosine_bitcast_fusion = (f32[64,2048]{1,0:T(8,128)S(1)}, f32[64,2048]{1,0:T(8,128)S(1)}) fusion(f32[32,2048]{1,0:T(8,128)S(1)} %copy-done.2, f32[32,64]{1,0:T(8,128)S(1)} %copy-done), kind=kOutput, calls=%fused_computation | convolution fusion | flops 50331648 | bytes 1318912 | tf_op jit(solution)/shard_map/ej,et->jt/dot_general | solution.py:406
  22.4 0.0 copy-done.1
  22.5 0.0 copy-done.6
  22.5 1.6 %shard_map.146.taps_ref = f32[17,64,256]{2,1,0:T(8,128)S(1)} custom-call(f32[64,2048]{1,0:T(8,128)S(1)} %get-tuple-element.23.hidden_ref, f32[64,128]{1,0:T(8,128)S(1)} %pad_maximum_fusion.params_ref, bf16[2,256,256]{2,1,0:T(8,128)(2,1)S(1)} %copy-done.1, f32[4,24,128]{2,1,0:T(8,128)S(1)} %copy-done.6), custom_call_target="tpu_custom_call" | custom-call | tf_op jit(solution)/shard_map/pallas_call | solution.py:370
  24.1 22.5 %all-to-all-done.got_ref = bf16[16,128,128]{2,1,0:T(8,128)(2,1)S(1)} async-done(((bf16[16,128,128]{2,1,0:T(8,128)(2,1)}), bf16[16,128,128]{2,1,0:T(8,128)(2,1)S(1)}, u32[]{:S(2)}, u32[]{:S(2)}) %all-to-all-start) | async-done | bytes 524320 | tf_op jit(solution)/shard_map/all_to_all | solution.py:405
  46.6 4.7 %shard_map.147 = bf16[32,16,128]{2,1,0:T(8,128)(2,1)} custom-call(bf16[16,128,128]{2,1,0:T(8,128)(2,1)S(1)} %all-to-all-done.got_ref, f32[64,2048]{1,0:T(8,128)S(1)} %get-tuple-element.22.slope_ref, f32[32,2048]{1,0:T(8,128)S(1)} %copy-done.2, f32[64,128]{1,0:T(8,128)S(1)} %pad_maximum_fusion.params_ref, bf16[2,256,256]{2,1,0:T(8,128)(2,1)S(1)} %copy-done.1, ...), custom_call_target="tpu_custom_call" | custom-call | tf_op jit(solution)/shard_map/pallas_call | solution.py:370
  51.3 7.3 %all-to-all-start.1 = ((bf16[32,16,128]{2,1,0:T(8,128)(2,1)}), bf16[32,16,128]{2,1,0:T(8,128)(2,1)S(1)}, u32[]{:S(2)}, u32[]{:S(2)}) async-start(bf16[32,16,128]{2,1,0:T(8,128)(2,1)} %shard_map.147), calls=%async_computation.1 | async-start | bytes 262144 | tf_op jit(solution)/shard_map/all_to_all | solution.py:429
  58.6 4.8 %shard_map.148._ = bf16[16,144,128]{2,1,0:T(8,128)(2,1)} custom-call(bf16[16,128,128]{2,1,0:T(8,128)(2,1)S(1)} %all-to-all-done.got_ref, f32[17,64,256]{2,1,0:T(8,128)S(1)} %shard_map.146.taps_ref, bf16[2,256,256]{2,1,0:T(8,128)(2,1)S(1)} %copy-done.1, f32[4,24,128]{2,1,0:T(8,128)S(1)} %copy-done.6), custom_call_target="tpu_custom_call" | custom-call | tf_op jit(solution)/shard_map/pallas_call | solution.py:370
  63.4 3.0 %all-to-all-done.1.shares_ref = bf16[32,16,128]{2,1,0:T(8,128)(2,1)S(1)} async-done(((bf16[32,16,128]{2,1,0:T(8,128)(2,1)}), bf16[32,16,128]{2,1,0:T(8,128)(2,1)S(1)}, u32[]{:S(2)}, u32[]{:S(2)}) %all-to-all-start.1) | async-done | bytes 131104 | tf_op jit(solution)/shard_map/all_to_all | solution.py:429
  66.4 0.8 shard_map.149
  67.2 0.0 copy-start.3
  67.2 0.0 copy-start.4
  67.3 0.0 copy-start.5
  67.3 7.3 %all-to-all-start.2 = ((bf16[16,144,128]{2,1,0:T(8,128)(2,1)}), bf16[16,144,128]{2,1,0:T(8,128)(2,1)S(1)}, u32[]{:S(2)}, u32[]{:S(2)}) async-start(bf16[16,144,128]{2,1,0:T(8,128)(2,1)} %shard_map.149), calls=%async_computation.2 | async-start | bytes 1179648 | tf_op jit(solution)/shard_map/all_to_all | solution.py:448
  74.6 5.1 %shard_map.151 = f32[64,128]{1,0:T(8,128)S(1)} custom-call(bf16[16,128,128]{2,1,0:T(8,128)(2,1)S(1)} %all-to-all-done.got_ref, f32[64,2048]{1,0:T(8,128)S(1)} %get-tuple-element.23.hidden_ref, f32[64,128]{1,0:T(8,128)S(1)} %pad_maximum_fusion.params_ref, bf16[2,256,256]{2,1,0:T(8,128)(2,1)S(1)} %copy-done.1, f32[4,24,128]{2,1,0:T(8,128)S(1)} %copy-done.6), custom_call_target="tpu_custom_call" | custom-call | tf_op jit(solution)/shard_map/pallas_call | solution.py:370
  79.6 1.9 %collective-permute-start = (f32[64,128]{1,0:T(8,128)S(1)}, f32[64,128]{1,0:T(8,128)S(1)}, u32[]{:S(2)}, u32[]{:S(2)}) collective-permute-start(f32[64,128]{1,0:T(8,128)S(1)} %shard_map.151), channel_id=1, source_target_pairs={{0,128},{128,0},{256,384},{384,256},{1,129},{129,1},{257,385},{385... | collective-permute-start | bytes 98312 | tf_op jit(solution)/shard_map/ppermute | solution.py:383
  81.6 1.2 %collective-permute-done = f32[64,128]{1,0:T(8,128)S(1)} collective-permute-done((f32[64,128]{1,0:T(8,128)S(1)}, f32[64,128]{1,0:T(8,128)S(1)}, u32[]{:S(2)}, u32[]{:S(2)}) %collective-permute-start) | collective-permute-done | bytes 32800 | tf_op jit(solution)/shard_map/ppermute | solution.py:383
  82.8 2.9 %collective-permute-start.1 = (f32[64,128]{1,0:T(8,128)S(1)}, f32[64,128]{1,0:T(8,128)S(1)}, u32[]{:S(2)}, u32[]{:S(2)}) collective-permute-start(f32[64,128]{1,0:T(8,128)S(1)} %add.6), channel_id=1, source_target_pairs={{0,256},{128,384},{256,0},{384,128},{1,257},{129,385},{257,1},{385... | collective-permute-start | bytes 98312 | tf_op jit(solution)/shard_map/ppermute | solution.py:383
  85.7 4.4 %collective-permute-done.1 = f32[64,128]{1,0:T(8,128)S(1)} collective-permute-done((f32[64,128]{1,0:T(8,128)S(1)}, f32[64,128]{1,0:T(8,128)S(1)}, u32[]{:S(2)}, u32[]{:S(2)}) %collective-permute-start.1) | collective-permute-done | bytes 32800 | tf_op jit(solution)/shard_map/ppermute | solution.py:383
  90.1 0.0 copy-start.8
  90.1 0.6 slice_bitcast_fusion
  90.7 15.7 %all-to-all-done.2.got_ref = bf16[16,144,128]{2,1,0:T(8,128)(2,1)S(1)} async-done(((bf16[16,144,128]{2,1,0:T(8,128)(2,1)}), bf16[16,144,128]{2,1,0:T(8,128)(2,1)S(1)}, u32[]{:S(2)}, u32[]{:S(2)}) %all-to-all-start.2) | async-done | bytes 589856 | tf_op jit(solution)/shard_map/all_to_all | solution.py:448
  106.4 0.0 copy-done.3
  106.4 0.0 copy-done.4
  106.4 0.0 copy-done.5
  106.4 1.2 %shard_map.150 = (bf16[1,128,1024]{2,1,0:T(8,128)(2,1)}, bf16[1,128,1024]{2,1,0:T(8,128)(2,1)}, bf16[1,128,1024]{2,1,0:T(8,128)(2,1)}, f32[32,64]{1,0:T(8,128)}) custom-call(bf16[16,144,128]{2,1,0:T(8,128)(2,1)S(1)} %all-to-all-done.2.got_ref, bf16[1,128,1024]{2,1,0:T(8,128)(2,1)S(1)} %copy-done.3, bf16[1,128,1024]{2,1,0:T(8,128)(2,1)S(1)} %copy-done.4, ...), custom_call_target="tpu_custom_call" | custom-call | tf_op jit(solution)/shard_map/pallas_call | solution.py:370
  107.6 0.0 copy-done.8
  (2 shorter events, 0.0 us)
Async XLA Ops:
  0.6 17.9 %copy-start = (f32[32,64]{1,0:T(8,128)S(1)}, f32[32,64]{1,0:T(8,128)}, u32[]{:S(2)}) copy-start(f32[32,64]{1,0:T(8,128)} %param.14) | copy-start | bytes 24580
  0.6 17.9 %copy-start.2 = (f32[32,2048]{1,0:T(8,128)S(1)}, f32[32,2048]{1,0:T(8,128)}, u32[]{:S(2)}) copy-start(f32[32,2048]{1,0:T(8,128)} %constant.8.clone.features_ref) | copy-start | bytes 786436
  0.7 17.8 %copy-start.7 = (f32[64,64]{1,0:T(8,128)S(1)}, f32[64,64]{1,0:T(8,128)}, u32[]{:S(2)}) copy-start(f32[64,64]{1,0:T(8,128)} %param.15) | copy-start | bytes 49156
  0.7 17.7 %copy-start.9 = (f32[64]{0:T(128)S(1)}, f32[64]{0:T(128)}, u32[]{:S(2)}) copy-start(f32[64]{0:T(128)} %param.16) | copy-start | bytes 772
  3.0 19.5 %copy-start.1 = (bf16[2,256,256]{2,1,0:T(8,128)(2,1)S(1)}, bf16[2,256,256]{2,1,0:T(8,128)(2,1)}, u32[]{:S(2)}) copy-start(bf16[2,256,256]{2,1,0:T(8,128)(2,1)} %constant.6.clone.table_ref) | copy-start | bytes 786436
  3.0 19.5 %copy-start.6 = (f32[4,24,128]{2,1,0:T(8,128)S(1)}, f32[4,24,128]{2,1,0:T(8,128)}, u32[]{:S(2)}) copy-start(f32[4,24,128]{2,1,0:T(8,128)} %constant.7.clone.turns_ref) | copy-start | bytes 147460
  3.0 43.6 %all-to-all-start = ((bf16[16,128,128]{2,1,0:T(8,128)(2,1)}), bf16[16,128,128]{2,1,0:T(8,128)(2,1)S(1)}, u32[]{:S(2)}, u32[]{:S(2)}) async-start(bf16[16,128,128]{2,1,0:T(8,128)(2,1)} %shard_map.145), calls=%async_computation | async-start | bytes 1048576 | tf_op jit(solution)/shard_map/all_to_all | solution.py:405
  51.3 15.1 %all-to-all-start.1 = ((bf16[32,16,128]{2,1,0:T(8,128)(2,1)}), bf16[32,16,128]{2,1,0:T(8,128)(2,1)S(1)}, u32[]{:S(2)}, u32[]{:S(2)}) async-start(bf16[32,16,128]{2,1,0:T(8,128)(2,1)} %shard_map.147), calls=%async_computation.1 | async-start | bytes 262144 | tf_op jit(solution)/shard_map/all_to_all | solution.py:429
  67.2 39.2 %copy-start.3 = (bf16[1,128,1024]{2,1,0:T(8,128)(2,1)S(1)}, bf16[1,128,1024]{2,1,0:T(8,128)(2,1)}, u32[]{:S(2)}) copy-start(bf16[1,128,1024]{2,1,0:T(8,128)(2,1)} %key_ref.1) | copy-start | bytes 786436
  67.2 39.1 %copy-start.4 = (bf16[1,128,1024]{2,1,0:T(8,128)(2,1)S(1)}, bf16[1,128,1024]{2,1,0:T(8,128)(2,1)}, u32[]{:S(2)}) copy-start(bf16[1,128,1024]{2,1,0:T(8,128)(2,1)} %value_ref.1) | copy-start | bytes 786436
  67.3 39.1 %copy-start.5 = (bf16[1,128,1024]{2,1,0:T(8,128)(2,1)S(1)}, bf16[1,128,1024]{2,1,0:T(8,128)(2,1)}, u32[]{:S(2)}) copy-start(bf16[1,128,1024]{2,1,0:T(8,128)(2,1)} %grad_ref.1) | copy-start | bytes 786436
  67.3 39.1 %all-to-all-start.2 = ((bf16[16,144,128]{2,1,0:T(8,128)(2,1)}), bf16[16,144,128]{2,1,0:T(8,128)(2,1)S(1)}, u32[]{:S(2)}, u32[]{:S(2)}) async-start(bf16[16,144,128]{2,1,0:T(8,128)(2,1)} %shard_map.149), calls=%async_computation.2 | async-start | bytes 1179648 | tf_op jit(solution)/shard_map/all_to_all | solution.py:448
  79.6 3.1 %collective-permute-start = (f32[64,128]{1,0:T(8,128)S(1)}, f32[64,128]{1,0:T(8,128)S(1)}, u32[]{:S(2)}, u32[]{:S(2)}) collective-permute-start(f32[64,128]{1,0:T(8,128)S(1)} %shard_map.151), channel_id=1, source_target_pairs={{0,128},{128,0},{256,384},{384,256},{1,129},{129,1},{257,385},{385... | collective-permute-start | bytes 98312 | tf_op jit(solution)/shard_map/ppermute | solution.py:383
  82.8 7.3 %collective-permute-start.1 = (f32[64,128]{1,0:T(8,128)S(1)}, f32[64,128]{1,0:T(8,128)S(1)}, u32[]{:S(2)}, u32[]{:S(2)}) collective-permute-start(f32[64,128]{1,0:T(8,128)S(1)} %add.6), channel_id=1, source_target_pairs={{0,256},{128,384},{256,0},{384,128},{1,257},{129,385},{257,1},{385... | collective-permute-start | bytes 98312 | tf_op jit(solution)/shard_map/ppermute | solution.py:383
  90.1 17.5 %copy-start.8 = (f32[64,128]{1,0:T(8,128)}, f32[64,128]{1,0:T(8,128)S(1)}, u32[]{:S(2)}) copy-start(f32[64,128]{1,0:T(8,128)S(1)} %add.7) | copy-start | bytes 98308

commit v5 on v4

--- a/solution.py
+++ b/solution.py
@@ -152,7 +152,7 @@
 
 
 def forward_outer(load, rows, turns_ref, turned_ref):
-    @pl.loop(0, rows // 8, unroll=2)
+    @pl.loop(0, rows // 8, unroll=4)
     def _(step):
         where = pl.ds(pl.multiple_of(step * 8, 8), 8)
         bins = outer_bins([load(n, where) for n in range(BLOCKS)])
@@ -170,7 +170,7 @@
 
 
 def inverse_outer(back_ref, rows, turns_ref, store):
-    @pl.loop(0, rows // 8, unroll=2)
+    @pl.loop(0, rows // 8, unroll=4)
     def _(step):
         where = pl.ds(pl.multiple_of(step * 8, 8), 8)
         bins = {}

time: 108 us -> 108 us (level)
  no operation moved by 1% of the time
where the time goes in v5:
time: 108 us; the launch traced here: 107 us
  waiting for transfers between devices  46.8 us (43%)
  starting transfers between devices  34.8 us (32%)
  Pallas kernels  20.4 us (19%)
  matrix products  3.92 us (4%)
    all_to_all x1, waiting for transfers between devices, per_device(): got = lax.all_to_all(sent, 'seq', split_axis=0, concat_axis=0, tiled=True)  22.5 us
    pallas_call x7, Pallas kernels, call(): pl.pallas_call(kernel, out_shape=[jax.ShapeDtypeStruct(shape, dtype) for...  20.4 us
    all_to_all x1, waiting for transfers between devices, per_device(): lax.all_to_all(result, 'seq', split_axis=0, concat_axis=0, tiled=True)  15.8 us
    all_to_all x1, starting transfers between devices, per_device(): got = lax.all_to_all(sent, 'seq', split_axis=0, concat_axis=0, tiled=True)  15.4 us
    all_to_all x1, starting transfers between devices, per_device(): lax.all_to_all(shares, plane, split_axis=0, concat_axis=0, tiled=True)  7.32 us
    all_to_all x1, starting transfers between devices, per_device(): lax.all_to_all(result, 'seq', split_axis=0, concat_axis=0, tiled=True)  7.3 us
    ppermute x2, waiting for transfers between devices, swapped_sum(): lax.ppermute(value, axis, [(i, i ^ step) for i in range(size)])  5.57 us
    ppermute x2, starting transfers between devices, swapped_sum(): lax.ppermute(value, axis, [(i, i ^ step) for i in range(size)])  4.84 us
  transfers between devices with their start and end apart: 5, of which 5 were waited for; matrix products, arithmetic and copies ran while one was open for 4% of the time, Pallas kernels for 11%

profile of v5, /device:TPU:32, one launch (start us, length us, event | category | flops | bytes accessed | tf_op | source)
XLA Modules:
  0.0 107.5 jit_solution(10400031697093495916)
XLA Ops:
  0.6 0.0 copy-start
  0.6 0.0 copy-start.2
  0.7 0.0 copy-start.7
  0.7 0.0 copy-start.9
  0.7 2.3 %shard_map.145 = bf16[16,128,128]{2,1,0:T(8,128)(2,1)} custom-call(bf16[1,128,1024]{2,1,0:T(8,128)(2,1)} %query_hbm.1, bf16[1,128,1024]{2,1,0:T(8,128)(2,1)} %key_ref.1, bf16[1,128,1024]{2,1,0:T(8,128)(2,1)} %value_ref.1, bf16[1,128,1024]{2,1,0:T(8,128)(2,1)} %grad_ref.1), custom_call_target="tpu_custom_call" | custom-call | tf_op jit(solution)/shard_map/pallas_call | solution.py:370
  3.0 0.0 copy-start.1
  3.0 0.0 copy-start.6
  3.0 15.4 %all-to-all-start = ((bf16[16,128,128]{2,1,0:T(8,128)(2,1)}), bf16[16,128,128]{2,1,0:T(8,128)(2,1)S(1)}, u32[]{:S(2)}, u32[]{:S(2)}) async-start(bf16[16,128,128]{2,1,0:T(8,128)(2,1)} %shard_map.145), calls=%async_computation | async-start | bytes 1048576 | tf_op jit(solution)/shard_map/all_to_all | solution.py:405
  18.3 0.0 copy-done.9
  18.3 0.1 broadcast_in_dim.2
  18.4 0.0 copy-done.7
  18.4 0.1 pad_maximum_fusion.params_ref
  18.5 0.0 copy-done
  18.5 0.0 copy-done.2
  18.5 3.9 %cosine_bitcast_fusion = (f32[64,2048]{1,0:T(8,128)S(1)}, f32[64,2048]{1,0:T(8,128)S(1)}) fusion(f32[32,2048]{1,0:T(8,128)S(1)} %copy-done.2, f32[32,64]{1,0:T(8,128)S(1)} %copy-done), kind=kOutput, calls=%fused_computation | convolution fusion | flops 50331648 | bytes 1318912 | tf_op jit(solution)/shard_map/ej,et->jt/dot_general | solution.py:406
  22.4 0.0 copy-done.1
  22.5 0.0 copy-done.6
  22.5 1.6 %shard_map.146.taps_ref = f32[17,64,256]{2,1,0:T(8,128)S(1)} custom-call(f32[64,2048]{1,0:T(8,128)S(1)} %get-tuple-element.23.hidden_ref, f32[64,128]{1,0:T(8,128)S(1)} %pad_maximum_fusion.params_ref, bf16[2,256,256]{2,1,0:T(8,128)(2,1)S(1)} %copy-done.1, f32[4,24,128]{2,1,0:T(8,128)S(1)} %copy-done.6), custom_call_target="tpu_custom_call" | custom-call | tf_op jit(solution)/shard_map/pallas_call | solution.py:370
  24.1 22.5 %all-to-all-done.got_ref = bf16[16,128,128]{2,1,0:T(8,128)(2,1)S(1)} async-done(((bf16[16,128,128]{2,1,0:T(8,128)(2,1)}), bf16[16,128,128]{2,1,0:T(8,128)(2,1)S(1)}, u32[]{:S(2)}, u32[]{:S(2)}) %all-to-all-start) | async-done | bytes 524320 | tf_op jit(solution)/shard_map/all_to_all | solution.py:405
  46.6 4.6 %shard_map.147 = bf16[32,16,128]{2,1,0:T(8,128)(2,1)} custom-call(bf16[16,128,128]{2,1,0:T(8,128)(2,1)S(1)} %all-to-all-done.got_ref, f32[64,2048]{1,0:T(8,128)S(1)} %get-tuple-element.22.slope_ref, f32[32,2048]{1,0:T(8,128)S(1)} %copy-done.2, f32[64,128]{1,0:T(8,128)S(1)} %pad_maximum_fusion.params_ref, bf16[2,256,256]{2,1,0:T(8,128)(2,1)S(1)} %copy-done.1, ...), custom_call_target="tpu_custom_call" | custom-call | tf_op jit(solution)/shard_map/pallas_call | solution.py:370
  51.2 7.3 %all-to-all-start.1 = ((bf16[32,16,128]{2,1,0:T(8,128)(2,1)}), bf16[32,16,128]{2,1,0:T(8,128)(2,1)S(1)}, u32[]{:S(2)}, u32[]{:S(2)}) async-start(bf16[32,16,128]{2,1,0:T(8,128)(2,1)} %shard_map.147), calls=%async_computation.1 | async-start | bytes 262144 | tf_op jit(solution)/shard_map/all_to_all | solution.py:429
  58.5 4.8 %shard_map.148._ = bf16[16,144,128]{2,1,0:T(8,128)(2,1)} custom-call(bf16[16,128,128]{2,1,0:T(8,128)(2,1)S(1)} %all-to-all-done.got_ref, f32[17,64,256]{2,1,0:T(8,128)S(1)} %shard_map.146.taps_ref, bf16[2,256,256]{2,1,0:T(8,128)(2,1)S(1)} %copy-done.1, f32[4,24,128]{2,1,0:T(8,128)S(1)} %copy-done.6), custom_call_target="tpu_custom_call" | custom-call | tf_op jit(solution)/shard_map/pallas_call | solution.py:370
  63.3 3.0 %all-to-all-done.1.shares_ref = bf16[32,16,128]{2,1,0:T(8,128)(2,1)S(1)} async-done(((bf16[32,16,128]{2,1,0:T(8,128)(2,1)}), bf16[32,16,128]{2,1,0:T(8,128)(2,1)S(1)}, u32[]{:S(2)}, u32[]{:S(2)}) %all-to-all-start.1) | async-done | bytes 131104 | tf_op jit(solution)/shard_map/all_to_all | solution.py:429
  66.3 0.8 shard_map.149
  67.2 0.0 copy-start.3
  67.2 0.0 copy-start.4
  67.2 0.0 copy-start.5
  67.2 7.3 %all-to-all-start.2 = ((bf16[16,144,128]{2,1,0:T(8,128)(2,1)}), bf16[16,144,128]{2,1,0:T(8,128)(2,1)S(1)}, u32[]{:S(2)}, u32[]{:S(2)}) async-start(bf16[16,144,128]{2,1,0:T(8,128)(2,1)} %shard_map.149), calls=%async_computation.2 | async-start | bytes 1179648 | tf_op jit(solution)/shard_map/all_to_all | solution.py:448
  74.5 5.0 %shard_map.151 = f32[64,128]{1,0:T(8,128)S(1)} custom-call(bf16[16,128,128]{2,1,0:T(8,128)(2,1)S(1)} %all-to-all-done.got_ref, f32[64,2048]{1,0:T(8,128)S(1)} %get-tuple-element.23.hidden_ref, f32[64,128]{1,0:T(8,128)S(1)} %pad_maximum_fusion.params_ref, bf16[2,256,256]{2,1,0:T(8,128)(2,1)S(1)} %copy-done.1, f32[4,24,128]{2,1,0:T(8,128)S(1)} %copy-done.6), custom_call_target="tpu_custom_call" | custom-call | tf_op jit(solution)/shard_map/pallas_call | solution.py:370
  79.5 1.9 %collective-permute-start = (f32[64,128]{1,0:T(8,128)S(1)}, f32[64,128]{1,0:T(8,128)S(1)}, u32[]{:S(2)}, u32[]{:S(2)}) collective-permute-start(f32[64,128]{1,0:T(8,128)S(1)} %shard_map.151), channel_id=1, source_target_pairs={{0,128},{128,0},{256,384},{384,256},{1,129},{129,1},{257,385},{385... | collective-permute-start | bytes 98312 | tf_op jit(solution)/shard_map/ppermute | solution.py:383
  81.5 1.2 %collective-permute-done = f32[64,128]{1,0:T(8,128)S(1)} collective-permute-done((f32[64,128]{1,0:T(8,128)S(1)}, f32[64,128]{1,0:T(8,128)S(1)}, u32[]{:S(2)}, u32[]{:S(2)}) %collective-permute-start) | collective-permute-done | bytes 32800 | tf_op jit(solution)/shard_map/ppermute | solution.py:383
  82.7 2.9 %collective-permute-start.1 = (f32[64,128]{1,0:T(8,128)S(1)}, f32[64,128]{1,0:T(8,128)S(1)}, u32[]{:S(2)}, u32[]{:S(2)}) collective-permute-start(f32[64,128]{1,0:T(8,128)S(1)} %add.6), channel_id=1, source_target_pairs={{0,256},{128,384},{256,0},{384,128},{1,257},{129,385},{257,1},{385... | collective-permute-start | bytes 98312 | tf_op jit(solution)/shard_map/ppermute | solution.py:383
  85.6 4.4 %collective-permute-done.1 = f32[64,128]{1,0:T(8,128)S(1)} collective-permute-done((f32[64,128]{1,0:T(8,128)S(1)}, f32[64,128]{1,0:T(8,128)S(1)}, u32[]{:S(2)}, u32[]{:S(2)}) %collective-permute-start.1) | collective-permute-done | bytes 32800 | tf_op jit(solution)/shard_map/ppermute | solution.py:383
  90.0 0.0 copy-start.8
  90.0 0.6 slice_bitcast_fusion
  90.6 15.8 %all-to-all-done.2.got_ref = bf16[16,144,128]{2,1,0:T(8,128)(2,1)S(1)} async-done(((bf16[16,144,128]{2,1,0:T(8,128)(2,1)}), bf16[16,144,128]{2,1,0:T(8,128)(2,1)S(1)}, u32[]{:S(2)}, u32[]{:S(2)}) %all-to-all-start.2) | async-done | bytes 589856 | tf_op jit(solution)/shard_map/all_to_all | solution.py:448
  106.3 0.0 copy-done.3
  106.3 0.0 copy-done.4
  106.3 0.0 copy-done.5
  106.3 1.2 %shard_map.150 = (bf16[1,128,1024]{2,1,0:T(8,128)(2,1)}, bf16[1,128,1024]{2,1,0:T(8,128)(2,1)}, bf16[1,128,1024]{2,1,0:T(8,128)(2,1)}, f32[32,64]{1,0:T(8,128)}) custom-call(bf16[16,144,128]{2,1,0:T(8,128)(2,1)S(1)} %all-to-all-done.2.got_ref, bf16[1,128,1024]{2,1,0:T(8,128)(2,1)S(1)} %copy-done.3, bf16[1,128,1024]{2,1,0:T(8,128)(2,1)S(1)} %copy-done.4, ...), custom_call_target="tpu_custom_call" | custom-call | tf_op jit(solution)/shard_map/pallas_call | solution.py:370
  107.5 0.0 copy-done.8
  (2 shorter events, 0.0 us)
Async XLA Ops:
  0.6 17.9 %copy-start = (f32[32,64]{1,0:T(8,128)S(1)}, f32[32,64]{1,0:T(8,128)}, u32[]{:S(2)}) copy-start(f32[32,64]{1,0:T(8,128)} %param.14) | copy-start | bytes 24580
  0.6 17.9 %copy-start.2 = (f32[32,2048]{1,0:T(8,128)S(1)}, f32[32,2048]{1,0:T(8,128)}, u32[]{:S(2)}) copy-start(f32[32,2048]{1,0:T(8,128)} %constant.8.clone.features_ref) | copy-start | bytes 786436
  0.7 17.8 %copy-start.7 = (f32[64,64]{1,0:T(8,128)S(1)}, f32[64,64]{1,0:T(8,128)}, u32[]{:S(2)}) copy-start(f32[64,64]{1,0:T(8,128)} %param.15) | copy-start | bytes 49156
  0.7 17.7 %copy-start.9 = (f32[64]{0:T(128)S(1)}, f32[64]{0:T(128)}, u32[]{:S(2)}) copy-start(f32[64]{0:T(128)} %param.16) | copy-start | bytes 772
  3.0 19.5 %copy-start.1 = (bf16[2,256,256]{2,1,0:T(8,128)(2,1)S(1)}, bf16[2,256,256]{2,1,0:T(8,128)(2,1)}, u32[]{:S(2)}) copy-start(bf16[2,256,256]{2,1,0:T(8,128)(2,1)} %constant.6.clone.table_ref) | copy-start | bytes 786436
  3.0 19.5 %copy-start.6 = (f32[4,24,128]{2,1,0:T(8,128)S(1)}, f32[4,24,128]{2,1,0:T(8,128)}, u32[]{:S(2)}) copy-start(f32[4,24,128]{2,1,0:T(8,128)} %constant.7.clone.turns_ref) | copy-start | bytes 147460
  3.0 43.6 %all-to-all-start = ((bf16[16,128,128]{2,1,0:T(8,128)(2,1)}), bf16[16,128,128]{2,1,0:T(8,128)(2,1)S(1)}, u32[]{:S(2)}, u32[]{:S(2)}) async-start(bf16[16,128,128]{2,1,0:T(8,128)(2,1)} %shard_map.145), calls=%async_computation | async-start | bytes 1048576 | tf_op jit(solution)/shard_map/all_to_all | solution.py:405
  51.2 15.1 %all-to-all-start.1 = ((bf16[32,16,128]{2,1,0:T(8,128)(2,1)}), bf16[32,16,128]{2,1,0:T(8,128)(2,1)S(1)}, u32[]{:S(2)}, u32[]{:S(2)}) async-start(bf16[32,16,128]{2,1,0:T(8,128)(2,1)} %shard_map.147), calls=%async_computation.1 | async-start | bytes 262144 | tf_op jit(solution)/shard_map/all_to_all | solution.py:429
  67.2 39.2 %copy-start.3 = (bf16[1,128,1024]{2,1,0:T(8,128)(2,1)S(1)}, bf16[1,128,1024]{2,1,0:T(8,128)(2,1)}, u32[]{:S(2)}) copy-start(bf16[1,128,1024]{2,1,0:T(8,128)(2,1)} %key_ref.1) | copy-start | bytes 786436
  67.2 39.1 %copy-start.4 = (bf16[1,128,1024]{2,1,0:T(8,128)(2,1)S(1)}, bf16[1,128,1024]{2,1,0:T(8,128)(2,1)}, u32[]{:S(2)}) copy-start(bf16[1,128,1024]{2,1,0:T(8,128)(2,1)} %value_ref.1) | copy-start | bytes 786436
  67.2 39.1 %copy-start.5 = (bf16[1,128,1024]{2,1,0:T(8,128)(2,1)S(1)}, bf16[1,128,1024]{2,1,0:T(8,128)(2,1)}, u32[]{:S(2)}) copy-start(bf16[1,128,1024]{2,1,0:T(8,128)(2,1)} %grad_ref.1) | copy-start | bytes 786436
  67.2 39.1 %all-to-all-start.2 = ((bf16[16,144,128]{2,1,0:T(8,128)(2,1)}), bf16[16,144,128]{2,1,0:T(8,128)(2,1)S(1)}, u32[]{:S(2)}, u32[]{:S(2)}) async-start(bf16[16,144,128]{2,1,0:T(8,128)(2,1)} %shard_map.149), calls=%async_computation.2 | async-start | bytes 1179648 | tf_op jit(solution)/shard_map/all_to_all | solution.py:448
  79.5 3.1 %collective-permute-start = (f32[64,128]{1,0:T(8,128)S(1)}, f32[64,128]{1,0:T(8,128)S(1)}, u32[]{:S(2)}, u32[]{:S(2)}) collective-permute-start(f32[64,128]{1,0:T(8,128)S(1)} %shard_map.151), channel_id=1, source_target_pairs={{0,128},{128,0},{256,384},{384,256},{1,129},{129,1},{257,385},{385... | collective-permute-start | bytes 98312 | tf_op jit(solution)/shard_map/ppermute | solution.py:383
  82.7 7.3 %collective-permute-start.1 = (f32[64,128]{1,0:T(8,128)S(1)}, f32[64,128]{1,0:T(8,128)S(1)}, u32[]{:S(2)}, u32[]{:S(2)}) collective-permute-start(f32[64,128]{1,0:T(8,128)S(1)} %add.6), channel_id=1, source_target_pairs={{0,256},{128,384},{256,0},{384,128},{1,257},{129,385},{257,1},{385... | collective-permute-start | bytes 98312 | tf_op jit(solution)/shard_map/ppermute | solution.py:383
  90.0 17.5 %copy-start.8 = (f32[64,128]{1,0:T(8,128)}, f32[64,128]{1,0:T(8,128)S(1)}, u32[]{:S(2)}) copy-start(f32[64,128]{1,0:T(8,128)S(1)} %add.7) | copy-start | bytes 98308
